TPU v7x, 32 devices: a whole 2x2x4 slice. The times are simulated.
32 devices in a mesh: layer: 2 (over core), expert: 4 (over y, x), matrix: 4 (over z).
Axes of the slice: x: 2, y: 2, z: 4, core: 2. Of those that a mesh axis runs over, the one named last changes fastest.
Arguments:
- grads: float32 [8, 1, 2048, 768], P(('layer', 'expert'), None, 'matrix'), parts along dimension 0, may hold values from -6 to 6
- basis_out: float32 [8, 2048, 2048], P('layer', None, ('expert', 'matrix')), parts along dimension 0, may hold values from -0.125 to 0.125
- basis_in: float32 [8, 768, 768], P('layer', ('expert', 'matrix')), parts along dimension 0, may hold values from -0.21875 to 0.21875
- eigvals: float32 [8, 2048, 768], P('layer', ('expert', 'matrix')), parts along dimension 0, may hold values from 0.001 to 1
- counts: int32 [8], P(('layer', 'expert')), parts along dimension 0, may hold values from 0 to 1, as said below
- slot_query: int32 [8, 1], P(('layer', 'expert')), parts along dimension 0, may hold values from 0 to 31
Outputs:
- precond: float32 [8, 1, 2048, 768], P(('layer', 'expert'), None, 'matrix'), parts along dimension 0
- scores: float32 [64], P('layer'), parts along dimension 0
There are 2 independent parts, one for each index of `layer`. A program takes and returns all parts, laid end to end along the dimension named above; each array names one. Nothing has to cross between parts.
Inputs may be any that keep to these rules, and one draw needn't show every extreme that they name: `counts`: some expert has no live slot and some expert has all 1.
All inputs are finite; a program needn't handle non-finite values.
Results may differ from a plain program's by a relative error of at most 0.0003.
Values sent between devices are 32-bit elements; how exact they have to be, the bound alone decides.
No kernel may reach another device: no remote copies, remote signals or barrier semaphores. Data moves between devices by JAX's collectives and lax.ppermute only.
A program may use at most 64 MiB of HBM per device.

v0:
```python
import jax
import jax.numpy as jnp
from jax import lax
from jax.sharding import PartitionSpec as P

QUERIES = 32


damping_fixed = 0.05
highest = lax.Precision.HIGHEST


def shards(grads, basis_out, basis_in, eigvals, counts, slot_query):
    capacity = grads.shape[1]
    own_rows = grads.shape[2]
    in_width = grads.shape[3]
    groups = lax.axis_size("matrix")
    columns = lax.all_to_all(basis_out, "expert", split_axis=0, concat_axis=2, tiled=True)[0]
    pieces = lax.all_gather(basis_in, "matrix", axis=1, tiled=True)
    scales, inner = (
        lax.all_to_all(eigvals, "expert", split_axis=0, concat_axis=1, tiled=True),
        lax.all_to_all(pieces, "expert", split_axis=0, concat_axis=1, tiled=True),
    )
    inner = inner[0]
    divisor = scales[0] + damping_fixed
    live_count = counts[0]
    queries = slot_query[0]
    local_rows = grads[0]
    slot_ids = jnp.arange(capacity, dtype=jnp.int32)
    live = (slot_ids < live_count).astype(jnp.float32)
    rotated = jnp.einsum(
        "ik,if->kf",
        columns,
        lax.all_gather(local_rows[0], "matrix", axis=0, tiled=True),
        precision=highest,
    )
    rotated = jnp.dot(rotated, inner, precision=highest)
    scaled = rotated / divisor
    back = jnp.einsum("kg,hg->kh", scaled, inner, precision=highest)

    def project_one(start, amount, back=back):
        return jnp.dot(columns, back, precision=highest)

    result = lax.psum_scatter(
        project_one(jnp.int32(0), own_rows * lax.axis_size("matrix")),
        "matrix",
        scatter_dimension=0,
        tiled=True,
    )
    results = [result * live[0]]
    precond = jnp.stack(results)
    values = jnp.sum(local_rows * precond, axis=(1, 2)) / (own_rows * groups * in_width)
    targets = jnp.arange(QUERIES, dtype=jnp.int32)
    onehot = (queries[:, None] == targets[None, :]).astype(jnp.float32)
    partial_scores = jnp.sum(values[:, None] * onehot, axis=0)
    scores = lax.psum(partial_scores, ("expert", "matrix"))
    return (precond[None], scores)


def solution(mesh):
    in_specs = (
        P(("layer", "expert"), None, "matrix", None),
        P("layer", None, ("expert", "matrix")),
        P("layer", ("expert", "matrix"), None),
        P("layer", ("expert", "matrix"), None),
        P(("layer", "expert")),
        P(("layer", "expert"), None),
    )
    out_specs = (P(("layer", "expert"), None, "matrix", None), P("layer"))
    return jax.shard_map(shards, mesh=mesh, in_specs=in_specs, out_specs=out_specs, check_vma=False)
```

profile of v0, /device:TPU:0, one launch (start us, length us, event | category | flops | bytes accessed | tf_op | source)
XLA Modules:
  0.0 377.7 jit_solution(351290143711426480)
XLA Ops:
  7.2 0.0 all-gather.4.cloned.1.call-start
  7.2 0.7 all-gather.4.cloned.1.call-update
  7.9 0.0 all-gather.6.cloned.1.call-start
  7.9 0.7 all-gather.6.cloned.1.call-update
  8.6 5.2 %all-to-all-start.2 = ((f32[4,128,768]{2,1,0:T(8,128)}), f32[4,128,768]{2,1,0:T(8,128)S(1)}, u32[]{:S(2)}, u32[]{:S(2)}) async-start(f32[4,128,768]{2,1,0:T(8,128)} %param.9), calls=%async_computation.2 | async-start | bytes 3145728 | tf_op jit(solution)/shard_map/all_to_all | solution.py:21
  13.8 5.4 %copy.10 = f32[4,2048,128]{1,2,0:T(8,128)} copy(f32[4,2048,128]{2,1,0:T(8,128)} %param.7) | data formatting | bytes 8388608 | tf_op args[1]
  19.2 13.9 %all-to-all-done.2 = f32[4,128,768]{2,1,0:T(8,128)S(1)} async-done(((f32[4,128,768]{2,1,0:T(8,128)}), f32[4,128,768]{2,1,0:T(8,128)S(1)}, u32[]{:S(2)}, u32[]{:S(2)}) %all-to-all-start.2) | async-done | bytes 1572896 | tf_op jit(solution)/shard_map/all_to_all | solution.py:21
  33.1 0.0 copy-start.2
  33.1 53.1 %all_to_all.33 = f32[4,2048,128]{1,2,0:T(8,128)} all-to-all(f32[4,2048,128]{1,2,0:T(8,128)} %copy.10), channel_id=1, replica_groups=mesh['layer'=2,'expert'=4,'matrix'=4] {'expert'}, dimensions={0} | all-to-all | bytes 8388608 | tf_op jit(solution)/shard_map/all_to_all | solution.py:18
  86.2 0.0 copy-done.2
  86.2 0.0 all-gather.4.cloned.1.call-done
  86.2 3.6 all-to-all-start.1
  89.8 0.0 reduce-scatter.2.cloned.1.call-start
  89.9 2.7 broadcast_add_fusion
  92.6 85.9 %all-gather.6.cloned.1.call-done = f32[1,1,2048,768]{3,2,1,0:T(8,128)} async-done(((f32[1,1,512,768]{3,2,1,0:T(8,128)}), f32[1,1,2048,768]{3,2,1,0:T(8,128)}) %all-gather.6.cloned.1.call-update) | async-done | bytes 6291472 | tf_op jit(solution)/shard_map/all_gather | solution.py:34
  178.6 14.2 %fusion = f32[512,768]{1,0:T(8,128)} fusion(f32[2048,512]{0,1:T(8,128)} %bitcast.31, f32[1,1,2048,768]{3,2,1,0:T(8,128)} %all-gather.6.cloned.1.call-done), kind=kOutput, calls=%fused_computation | convolution fusion | flops 9663676416 | bytes 12058624 | tf_op jit(solution)/shard_map/ik,if->kf/dot_general | solution.py:31
  192.7 0.0 all-to-all-done.1
  192.8 5.9 %bitcast_divide_fusion = f32[512,768]{1,0:T(8,128)S(1)} fusion(f32[4,128,768]{2,1,0:T(8,128)} %broadcast_add_fusion, f32[512,768]{1,0:T(8,128)} %fusion, f32[768,768]{1,0:T(8,128)S(1)} %bitcast.29), kind=kOutput, calls=%fused_computation.5 | convolution fusion | flops 3624271872 | bytes 7077888 | tf_op jit(solution)/shard_map/dot_general | solution.py:37
  198.7 0.0 copy-start
  198.7 4.0 %fusion.3 = f32[512,768]{1,0:T(8,128)S(1)} fusion(f32[512,768]{1,0:T(8,128)S(1)} %bitcast_divide_fusion, f32[768,768]{1,0:T(8,128)S(1)} %bitcast.30), kind=kOutput, calls=%fused_computation.9 | convolution fusion | flops 3623878656 | bytes 5505024 | tf_op jit(solution)/shard_map/kg,hg->kh/dot_general | solution.py:39
  202.7 0.0 copy-done
  202.8 12.6 %convolution_bitcast_fusion = f32[2048,768]{0,1:T(8,128)} fusion(f32[512,768]{1,0:T(8,128)S(1)} %fusion.3, f32[2048,512]{0,1:T(8,128)S(1)} %bitcast.32), kind=kOutput, calls=%fused_computation.2 | convolution fusion | flops 9663676416 | bytes 12058624 | tf_op jit(solution)/shard_map/dot_general | solution.py:42
  215.3 0.0 copy-start.1
  215.3 0.0 reduce-scatter.2.cloned.1.call-update
  215.4 1.4 copy-done.1
  216.8 0.5 copy.11
  218.5 106.0 %reduce-scatter.2.cloned.1.call-done = f32[512,768]{0,1:T(8,128)} async-done(((f32[2048,768]{0,1:T(8,128)}), f32[512,768]{0,1:T(8,128)}) %reduce-scatter.2.cloned.1.call-update) | async-done | bytes 1572880 | tf_op jit(solution)/shard_map/reduce_scatter | solution.py:44
  324.5 2.5 fusion.2
  327.0 1.6 copy.12
  329.3 41.9 %psum.7 = f32[32]{0:T(128)} all-reduce(f32[32]{0:T(128)S(1)} %compare_select_fusion), channel_id=1, replica_groups=mesh['layer'=2,'expert'=4,'matrix'=4] {'expert','matrix'}, use_global_device_ids=true, to_apply=%region_2.0 | all-reduce | flops 32 | bytes 256 | tf_op jit(solution)/shard_map/psum | solution.py:56
  (1 shorter events, 0.0 us)
Async XLA Ops:
  7.2 79.0 %all-gather.4.cloned.1.call-start = ((), (), s32[]{:S(2)}) async-start(), calls=%async_computation.4 | async-start | bytes 2949120 | tf_op jit(solution)/shard_map/all_gather | solution.py:19
  7.9 170.7 %all-gather.6.cloned.1.call-start = ((), (), s32[]{:S(2)}) async-start(), calls=%async_computation.6 | async-start | bytes 7864320 | tf_op jit(solution)/shard_map/all_gather | solution.py:34
  8.6 24.4 %all-to-all-start.2 = ((f32[4,128,768]{2,1,0:T(8,128)}), f32[4,128,768]{2,1,0:T(8,128)S(1)}, u32[]{:S(2)}, u32[]{:S(2)}) async-start(f32[4,128,768]{2,1,0:T(8,128)} %param.9), calls=%async_computation.2 | async-start | bytes 3145728 | tf_op jit(solution)/shard_map/all_to_all | solution.py:21
  33.1 53.1 %copy-start.2 = (f32[4,128,768]{2,1,0:T(8,128)}, f32[4,128,768]{2,1,0:T(8,128)S(1)}, u32[]{:S(2)}) copy-start(f32[4,128,768]{2,1,0:T(8,128)S(1)} %all-to-all-done.2) | copy-start | bytes 4718596
  86.2 106.6 %all-to-all-start.1 = ((f32[4,192,768]{2,1,0:T(8,128)}), f32[4,192,768]{2,1,0:T(8,128)S(1)}, u32[]{:S(2)}, u32[]{:S(2)}) async-start(f32[4,192,768]{2,1,0:T(8,128)} %all-gather.4.cloned.1.call-done), calls=%async_computation.1 | async-start | bytes 4718592 | tf_op jit(solution)/shard_map/all_to_all | solution.py:22
  89.8 234.7 %reduce-scatter.2.cloned.1.call-start = ((), (), s32[]{:S(2)}) async-start(), calls=%async_computation.5 | async-start | bytes 7864320 | tf_op jit(solution)/shard_map/reduce_scatter | solution.py:44
  198.7 4.1 %copy-start = (f32[4,2048,128]{1,2,0:T(8,128)S(1)}, f32[4,2048,128]{1,2,0:T(8,128)}, u32[]{:S(2)}) copy-start(f32[4,2048,128]{1,2,0:T(8,128)} %all_to_all.33) | copy-start | bytes 12582916
  215.3 1.4 copy-start.1
Sparse Core Ops, SparseCore 0:
  9.6 53.1 all-gather.3
  64.3 114.1 all-gather.5
  215.5 108.9 reduce-scatter.1
where the time goes:
time: 378 us
  waiting for transfers between devices  207 us (55%)
  blocking collectives  95 us (25%)
  matrix products  36.8 us (10%)
  between operations  15.8 us (4%)
  starting transfers between devices  8.93 us (2%)
  local copies, waits for them, and re-layouts  8.87 us (2%)
  other arithmetic  5.24 us (1%)
    reduce_scatter x1, waiting for transfers between devices, shards(): lax.psum_scatter(project_one(jnp.int32(0), own_rows * lax.axis_size('matr...  106 us
    all_gather x1, waiting for transfers between devices, shards(): lax.all_gather(local_rows[0], 'matrix', axis=0, tiled=True)  85.9 us
    all_to_all x1, blocking collectives, shards(): lax.all_to_all(basis_out, 'expert', split_axis=0, concat_axis=2, tiled=True)  53.1 us
    psum x1, blocking collectives, shards(): scores = lax.psum(partial_scores, ('expert', 'matrix'))  41.9 us
    dot_general x1, matrix products, shards(): jnp.einsum('ik,if->kf', columns, lax.all_gather(local_rows[0], 'matrix',...  14.2 us
    all_to_all x1, waiting for transfers between devices, shards(): lax.all_to_all(eigvals, 'expert', split_axis=0, concat_axis=1, tiled=True)  13.9 us
    dot_general x1, matrix products, project_one(): return jnp.dot(columns, back, precision=highest)  12.6 us
    unnamed x9, local copies, waits for them, and re-layouts  8.87 us
  transfers between devices with their start and end apart: 5, of which 3 were waited for; matrix products, arithmetic and copies ran while one was open for 6% of the time, Pallas kernels for 0%

commit v1 on v0

v1 whole, which is shorter than its diff:
```python
import functools

import jax
import jax.numpy as jnp
from jax import lax
from jax.experimental import pallas as pl
from jax.experimental.pallas import tpu as pltpu
from jax.sharding import PartitionSpec as P

QUERIES = 32

damping_fixed = 0.05
F32 = jnp.float32
BF16 = jnp.bfloat16

IDLE, ONE_BLOCK, TWO_BLOCKS = 0, 1, 2


def split(x):
    high = x.astype(BF16)
    return high, (x - high.astype(F32)).astype(BF16)


def three_pass(a, b, contract):
    dims = (contract, ((), ()))
    dot = functools.partial(lax.dot_general, dimension_numbers=dims, preferred_element_type=F32)
    return dot(a[0], b[0]) + (dot(a[0], b[1]) + dot(a[1], b[0]))


def pack_kernel(experts, meta, outs, eigs, *refs):
    packed, sems = refs[:experts], refs[experts]
    depth, width = outs.shape[1], outs.shape[2]
    height = eigs.shape[1]
    chunks = eigs.shape[2] // width
    copies = []
    for distance in range(experts):
        target = lax.bitwise_xor(meta[2], distance)
        base = distance * (chunks + 1)
        copies.append(
            pltpu.make_async_copy(outs.at[target], packed[distance].at[pl.ds(0, depth), :], sems.at[base])
        )
        for chunk in range(chunks):
            copies.append(
                pltpu.make_async_copy(
                    eigs.at[target, :, pl.ds(chunk * width, width)],
                    packed[distance].at[pl.ds(depth + chunk * height, height), :],
                    sems.at[base + 1 + chunk],
                )
            )
    for copy in copies:
        copy.start()
    for copy in copies:
        copy.wait()


def pack(meta, outs, eigs):
    experts, depth, width = outs.shape
    chunks = eigs.shape[2] // width
    in_hbm = pl.BlockSpec(memory_space=pltpu.HBM)
    shape = jax.ShapeDtypeStruct((depth + chunks * eigs.shape[1], width), F32)
    return pl.pallas_call(
        functools.partial(pack_kernel, experts),
        out_shape=[shape] * experts,
        in_specs=[pl.BlockSpec(memory_space=pltpu.SMEM), in_hbm, in_hbm],
        out_specs=[pl.BlockSpec(memory_space=pltpu.VMEM)] * experts,
        scratch_shapes=[pltpu.SemaphoreType.DMA((experts * (chunks + 1),))],
        compiler_params=pltpu.CompilerParams(vmem_limit_bytes=32 * 1024 * 1024),
        cost_estimate=pl.CostEstimate(flops=0, bytes_accessed=8 * (outs.size + eigs.size), transcendentals=0),
        name="pack",
    )(meta, outs, eigs)


def block_kernel(planes, inner_job, second, n_own, n_piece, fused, meta, *refs):
    refs = list(refs)

    def take(number):
        taken, refs[:number] = refs[:number], []
        return taken

    hops = planes - 1
    here_refs = take(2 if fused else 1)
    near_up, near_down = take(2 if fused else 1), take(2 if fused else 1)
    far_up, far_down = take(hops - 1), take(hops - 1)
    own_refs, piece_refs = take(n_own), take(n_piece)
    in_refs = take(0 if fused else 1)
    earlier = take(2 * planes - 1) if second else None
    sums = take(2 * planes - 1)
    (energy,) = take(1)
    grad, cols, cols_high, cols_low, eig, inner, work, rotated, back_high, back_low, total = take(11)
    out_sems, eig_sems, grad_sems, in_sems, sum_sems = refs
    rows = grad.shape[1]
    here, role, expert, live = meta[0], meta[1], meta[2], meta[3]
    depth, block = cols.shape

    def relative(target, plane):
        if target < plane:
            return plane - target
        if target > plane:
            return hops + target - plane
        return 0

    def per_plane(action):
        for plane in range(planes):
            pl.when(here == plane)(functools.partial(action, plane))

    def per_plane_and_role(action):
        if not second:
            for plane in range(planes):
                pl.when((here == plane) & (role == ONE_BLOCK))(functools.partial(action, plane, False))
        if inner_job:
            for plane in (1, planes - 2):
                pl.when((here == plane) & (role == TWO_BLOCKS))(functools.partial(action, plane, True))

    def sources(target, plane, inner_only):
        distance = abs(target - plane)
        if distance == 0:
            return here_refs
        if distance == 1:
            return near_up if target < plane else near_down
        step = hops if inner_only else distance
        ref = (far_up if target < plane else far_down)[step - 2]
        if not fused:
            return [ref]
        return [ref.at[pl.ds(0, rows), :], ref.at[pl.ds(rows, ref.shape[0] - rows), :]]

    def compute():
        pieces = n_piece + (1 if n_own else 0)
        width = height = block // pieces
        out_copies, eig_copies = [], []

        def place(copies, sems, source, spot):
            copies.append(pltpu.make_async_copy(source, spot, sems.at[len(copies)]))

        owns = [ref.at[expert] if len(ref.shape) == 3 else ref for ref in own_refs]
        first = 1 if n_own else 0
        if n_own:
            place(out_copies, out_sems, owns[0], cols.at[:, pl.ds(0, width)])
            place(eig_copies, eig_sems, owns[1], eig.at[pl.ds(0, height), :])
        for index, ref in enumerate(piece_refs, first):
            place(out_copies, out_sems, ref.at[pl.ds(0, depth), :], cols.at[:, pl.ds(index * width, width)])
            for chunk in range(eig.shape[1] // width):
                spot = eig.at[pl.ds(index * height, height), pl.ds(chunk * width, width)]
                place(eig_copies, eig_sems, ref.at[pl.ds(depth + chunk * height, height), :], spot)
        for copy in out_copies:
            copy.start()

        in_copies = []

        def in_copy(target, distance, source):
            part = source.shape[0] // pieces
            owner = lax.bitwise_xor(expert, distance)
            to = pl.multiple_of((owner * planes + target) * part, part)
            window = source.at[pl.ds(distance * part, part), :]
            sem = in_sems.at[target * pieces + distance]
            return pltpu.make_async_copy(window, inner.at[pl.ds(to, part), :], sem)

        def start_shards(plane, inner_only):
            for target in range(planes):
                source = sources(target, plane, inner_only)[0]
                pltpu.make_async_copy(source, grad.at[target], grad_sems.at[target]).start()
            if fused:
                for target in range(planes):
                    source = sources(target, plane, inner_only)[1]
                    for distance in range(pieces):
                        in_copy(target, distance, source).start()

        per_plane_and_role(start_shards)
        if fused:
            in_copies += [in_copy(t, d, here_refs[1]) for t in range(planes) for d in range(pieces)]
        else:
            in_copies.append(pltpu.make_async_copy(in_refs[0], inner, in_sems.at[0]))
            in_copies[0].start()
        for copy in eig_copies:
            copy.start()
        if second:

            def start_earlier(plane):
                for target in range(planes):
                    source = earlier[relative(target, plane)]
                    pltpu.make_async_copy(source, total.at[target], sum_sems.at[target]).start()

            per_plane(start_earlier)

        for copy in out_copies:
            copy.wait()
        work[...] = jnp.zeros_like(work)

        @pl.loop(0, planes)
        def _(target):
            pltpu.make_async_copy(here_refs[0], grad.at[target], grad_sems.at[target]).wait()
            window = pl.ds(pl.multiple_of(target * rows, rows), rows)
            left = split(cols[window, :])
            cols_high[window, :] = left[0]
            cols_low[window, :] = left[1]
            work[...] += three_pass(left, split(grad[target]), ((0,), (0,)))

        for copy in in_copies:
            copy.wait()
        rotated[...] = three_pass(split(work[...]), split(inner[...]), ((1,), (0,)))
        for copy in eig_copies:
            copy.wait()
        alive = (live > 0).astype(F32)
        turned = rotated[...]
        scaled = turned / (eig[...] + damping_fixed) * alive
        work[...] = scaled
        energy[...] = jnp.sum(turned * scaled, axis=0, keepdims=True)
        high, low = split(three_pass(split(work[...]), split(inner[...]), ((1,), (1,))))
        back_high[...] = high
        back_low[...] = low

        def out_copy(target, plane):
            return pltpu.make_async_copy(
                total.at[target], sums[relative(target, plane)], sum_sems.at[planes + target]
            )

        for target in range(planes):
            window = pl.ds(target * rows, rows)
            product = three_pass(
                (cols_high[window, :], cols_low[window, :]), (back_high[...], back_low[...]), ((1,), (0,))
            )
            if second:
                pltpu.make_async_copy(earlier[0], total.at[target], sum_sems.at[target]).wait()
                total[target] += product
            else:
                total[target] = product
            per_plane(lambda plane, target=target: out_copy(target, plane).start())
        for target in range(planes):
            out_copy(target, target).wait()

    def idle():
        energy[...] = jnp.zeros_like(energy)
        if not second:
            total[0] = jnp.zeros_like(total[0])
            copy = pltpu.make_async_copy(total.at[0], sums[0], sum_sems.at[0])
            copy.start()
            copy.wait()

    least = TWO_BLOCKS if second else ONE_BLOCK
    pl.when(role >= least)(compute)
    pl.when(role < least)(idle)


def run_block(planes, block, inner_job, meta, shards, owns, pieces, inners, earlier=None):
    second = earlier is not None
    rows, width = shards[0].shape
    operands = [*shards, *owns, *pieces, *inners, *(earlier or [])]
    in_hbm = pl.BlockSpec(memory_space=pltpu.HBM)
    sums = [jax.ShapeDtypeStruct((rows, width), F32)] * (2 * planes - 1)
    first_alias = 1 + len(operands) - len(sums)
    number = len(pieces) + (1 if owns else 0)
    dma = pltpu.SemaphoreType.DMA
    flops = 2 * block * width * (2 * rows * planes + 2 * width)
    results = pl.pallas_call(
        functools.partial(block_kernel, planes, inner_job, second, len(owns), len(pieces), not inners),
        out_shape=[*sums, jax.ShapeDtypeStruct((1, width), F32)],
        in_specs=[pl.BlockSpec(memory_space=pltpu.SMEM)] + [in_hbm] * len(operands),
        out_specs=[in_hbm] * len(sums) + [pl.BlockSpec(memory_space=pltpu.VMEM)],
        scratch_shapes=[
            pltpu.VMEM((planes, rows, width), F32),
            pltpu.VMEM((planes * rows, block), F32),
            pltpu.VMEM((planes * rows, block), BF16),
            pltpu.VMEM((planes * rows, block), BF16),
            pltpu.VMEM((block, width), F32),
            pltpu.VMEM((width, width), F32),
            pltpu.VMEM((block, width), F32),
            pltpu.VMEM((block, width), F32),
            pltpu.VMEM((block, width), BF16),
            pltpu.VMEM((block, width), BF16),
            pltpu.VMEM((planes, rows, width), F32),
            dma((number,)),
            dma((1 + number * max(1, width * number // block),)),
            dma((planes,)),
            dma((planes * number,)),
            dma((2 * planes,)),
        ],
        input_output_aliases={first_alias + i: i for i in range(len(sums))} if second else {},
        cost_estimate=pl.CostEstimate(flops=3 * flops, bytes_accessed=4 * 5 * rows * planes * width, transcendentals=0),
        compiler_params=pltpu.CompilerParams(vmem_limit_bytes=56 * 1024 * 1024),
        name="second_block" if second else "first_block",
    )(meta, *operands)
    return results[:-1], results[-1]


def shards(grads, basis_out, basis_in, eigvals, counts, slot_query):
    experts = lax.axis_size("expert")
    planes = lax.axis_size("matrix")
    layers = lax.axis_size("layer")
    expert = lax.axis_index("expert")
    here = lax.axis_index("matrix")
    layer = lax.axis_index("layer")
    rows, width = grads.shape[2], grads.shape[3]
    depth = rows * planes
    last = planes - 1
    inward = [l == 0 and layers == 2 and planes == 4 for l in range(layers)]

    takes_over = jnp.asarray(inward)[layer]
    at_end = (here == 0) | (here == last)
    role = jnp.where(takes_over, jnp.where(at_end, IDLE, TWO_BLOCKS), ONE_BLOCK)
    meta = jnp.stack([here, role, expert, counts[0]]).astype(jnp.int32)

    def move(x, pairs):
        return lax.ppermute(x, ("layer", "matrix"), [(l * planes + a, l * planes + b) for l, a, b in pairs])

    def mirror(pairs):
        return [(l, last - a, last - b) for l, a, b in pairs]

    def gather_pairs(step):
        pairs = [(l, a, a + 1) for l in range(layers) if not inward[l] for a in range(step - 1, last)]
        if step == 1:
            pairs += [(l, a, a + 1) for l in range(layers) if inward[l] for a in range(last - 1)]
        if step == last:
            pairs += [(l, 1, last - 1) for l in range(layers) if inward[l]]
        return pairs

    def reduce_pairs(step):
        low = [1 if inward[l] else 0 for l in range(layers)]
        return [(l, a, a + 1) for l in range(layers) for a in range(low[l], step)]

    def token(x, y):
        mark = x[:8, :128] + y[:8, :128]
        return lax.ppermute(mark, ("layer", "matrix"), [(planes + m, m) for m in range(planes)])

    def near(x):
        return move(x, gather_pairs(1)), move(x, mirror(gather_pairs(1)))

    def far(below, above, ties):
        ups, downs = [below], [above]
        for step in range(2, planes):
            up, down = ups[-1], downs[-1]
            before = list(ties.get(step, ()))
            if any(inward) and step == last:
                before.append(token(up, down))
                up = jnp.where(takes_over, below, up)
                down = jnp.where(takes_over, above, down)
            (up, down), _ = lax.optimization_barrier(((up, down), before))
            ups.append(move(up, gather_pairs(step)))
            downs.append(move(down, mirror(gather_pairs(step))))
        return ups[1:], downs[1:]

    columns, heights = basis_out.shape[2], eigvals.shape[1]
    block = experts * columns
    fits = columns % 128 == 0 and width % columns == 0 and columns == heights
    fits = fits and basis_in.shape[1] % 8 == 0 and experts & (experts - 1) == 0

    def index(l, e, m):
        return (l * experts + e) * planes + m

    def goes_over(l, m):
        return inward[l] and m in (0, last)

    def crossing(x, distance, chosen, turn=lambda m: m):
        every = [(l, e, m) for l in range(layers) for e in range(experts) for m in range(planes)]
        pairs = [(index(l, e, m), index(l, e ^ distance, turn(m))) for l, e, m in every if chosen(l, m)]
        return lax.ppermute(x, ("layer", "expert", "matrix"), pairs)

    own = grads[0, 0]
    own_up, own_down = near(own)
    if fits:
        parts = [
            lax.dynamic_index_in_dim(basis_in, lax.bitwise_xor(expert, distance), 0, keepdims=False)
            for distance in range(experts)
        ]
        parts = [x if d == 0 else crossing(x, d, lambda l, m: True) for d, x in enumerate(parts)]
        packed = pack(meta, basis_out, eigvals)
        parts, packed = lax.optimization_barrier((parts, packed))
        pieces = [crossing(packed[d], d, lambda l, m: not goes_over(l, m)) for d in range(1, experts)]
        over = []
        if any(inward):
            packed, _ = lax.optimization_barrier((packed, (own_up, own_down)))
            over = [crossing(packed[d], d, goes_over, lambda m: 1 if m == 0 else last - 1) for d in range(experts)]
        part = jnp.concatenate(parts)
        part_up, part_down = near(part)
        ties = {2: pieces[:-1], 3: [*pieces[-1:], *over[:1]]}
        below, above = far(jnp.concatenate([own_up, part_up]), jnp.concatenate([own_down, part_down]), ties)
        near_shards = [own, part, own_up, part_up, own_down, part_down]
        first_owns, first_pieces, inners = [basis_out, eigvals], pieces, []
    else:
        eig = lax.all_to_all(eigvals, "expert", split_axis=0, concat_axis=1, tiled=True)[0]
        out = lax.all_to_all(basis_out, "expert", split_axis=0, concat_axis=2, tiled=True)[0]
        inner = lax.all_gather(basis_in, "matrix", axis=1, tiled=True)
        inner = lax.all_to_all(inner, "expert", split_axis=0, concat_axis=0, tiled=True).reshape(width, width)
        below, above = far(own_up, own_down, {})
        near_shards = [own, own_up, own_down]
        first_owns, first_pieces, inners = [out, eig], [], [inner]

    shards_of_job = [*near_shards, *below, *above]
    sums, energy = run_block(planes, block, any(inward), meta, shards_of_job, first_owns, first_pieces, inners)
    if any(inward):
        second_owns, second_pieces = [], []
        if fits:
            second_pieces = over
        else:
            ends = [pair for l in range(layers) if inward[l] for pair in ((l, 0, 1), (l, last, last - 1))]
            second_owns = [move(x, ends) for x in first_owns]
        sums, more = run_block(
            planes, block, True, meta, shards_of_job, second_owns, second_pieces, inners, sums
        )
        energy = energy + more

    below, above = sums[1:planes], sums[planes:]

    def spread(partials, turn):
        moved = None
        for step in range(1, planes):
            partial = partials[last - step]
            moved = move(partial if moved is None else partial + moved, turn(reduce_pairs(step)))
        return moved

    result = sums[0] + (spread(above, lambda pairs: pairs) + spread(below, mirror))

    value = jnp.sum(energy) / (depth * width)
    scores = jnp.where(jnp.arange(QUERIES, dtype=jnp.int32) == slot_query[0, 0], value, 0.0)
    for axis, size in (("expert", experts), ("matrix", planes)):
        if size & (size - 1):
            scores = lax.psum(scores, axis)
            continue
        distance = 1
        while distance < size:
            scores = scores + lax.ppermute(scores, axis, [(i, i ^ distance) for i in range(size)])
            distance *= 2
    return (result[None, None], scores)


def solution(mesh):
    in_specs = (
        P(("layer", "expert"), None, "matrix", None),
        P("layer", None, ("expert", "matrix")),
        P("layer", ("expert", "matrix"), None),
        P("layer", ("expert", "matrix"), None),
        P(("layer", "expert")),
        P(("layer", "expert"), None),
    )
    out_specs = (P(("layer", "expert"), None, "matrix", None), P("layer"))
    return jax.shard_map(shards, mesh=mesh, in_specs=in_specs, out_specs=out_specs, check_vma=False)
```

time: 378 us -> 263 us (0.70)
  starting transfers between devices: 8.93 us -> 149 us
  waiting for transfers between devices: 207 us -> 75.6 us
  blocking collectives: 95 us -> 0 us
  matrix products: 36.8 us -> 0 us
  between operations: 15.8 us -> 3.77 us
  local copies, waits for them, and re-layouts: 8.87 us -> 17.3 us
  Pallas kernels: 0 us -> 6.29 us
  other arithmetic: 5.24 us -> 9.88 us
    ppermute x0 -> x28, starting transfers between devices: none -> 149 us  [the longest x4 80.2 us: shards(): lax.ppermute(scores, axis, [(i, i ^ distance) for i in range(size)])]
    reduce_scatter x1 -> x0, waiting for transfers between devices: 106 us -> none  [shards(): lax.psum_scatter(project_one(jnp.int32(0), own_rows * lax.axis_size('matr...]
    all_gather x2 -> x0, waiting for transfers between devices: 85.9 us -> none  [the longest x1 85.9 us: shards(): lax.all_gather(local_rows[0], 'matrix', axis=0, tiled=True)]
    ppermute x0 -> x28, waiting for transfers between devices: none -> 75.6 us  [the longest x10 49.3 us: crossing(): return lax.ppermute(x, ('layer', 'expert', 'matrix'), pairs)]
    all_to_all x1 -> x0, blocking collectives: 53.1 us -> none  [shards(): lax.all_to_all(basis_out, 'expert', split_axis=0, concat_axis=2, tiled=True)]
    psum x1 -> x0, blocking collectives: 41.9 us -> none  [shards(): scores = lax.psum(partial_scores, ('expert', 'matrix'))]
    dot_general x4 -> x0, matrix products: 36.8 us -> none  [the longest x1 14.2 us: shards(): jnp.einsum('ik,if->kf', columns, lax.all_gather(local_rows[0], 'matrix',...]
    all_to_all x2 -> x0, waiting for transfers between devices: 13.9 us -> none  [the longest x1 13.9 us: shards(): lax.all_to_all(eigvals, 'expert', split_axis=0, concat_axis=1, tiled=True)]
  transfers between devices with their start and end apart: 5 -> 28, of which waited for: 3 -> 10; matrix products, arithmetic and copies ran while one was open for 6% -> 5% of each run, Pallas kernels for 0% -> 2%
where the time goes in v1:
time: 263 us; the launch traced here: 262 us
  starting transfers between devices  149 us (57%)
  waiting for transfers between devices  75.6 us (29%)
  local copies, waits for them, and re-layouts  17.3 us (7%)
  other arithmetic  9.88 us (4%)
  Pallas kernels  6.29 us (2%)
  between operations  3.77 us (1%)
    ppermute x4, starting transfers between devices, shards(): lax.ppermute(scores, axis, [(i, i ^ distance) for i in range(size)])  80.2 us
    ppermute x10, waiting for transfers between devices, crossing(): return lax.ppermute(x, ('layer', 'expert', 'matrix'), pairs)  49.3 us
    ppermute x10, starting transfers between devices, crossing(): return lax.ppermute(x, ('layer', 'expert', 'matrix'), pairs)  41.8 us
    ppermute x14, starting transfers between devices, move(): lax.ppermute(x, ('layer', 'matrix'), [(l * planes + a, l * planes + b) fo...  26.9 us
    ppermute x14, waiting for transfers between devices, move(): lax.ppermute(x, ('layer', 'matrix'), [(l * planes + a, l * planes + b) fo...  17.8 us
    unnamed x45, local copies, waits for them, and re-layouts  13.1 us
    ppermute x4, waiting for transfers between devices, shards(): lax.ppermute(scores, axis, [(i, i ^ distance) for i in range(size)])  8.45 us
  transfers between devices with their start and end apart: 28, of which 10 were waited for; matrix products, arithmetic and copies ran while one was open for 5% of the time, Pallas kernels for 2%

profile of v1, /device:TPU:0, one launch (start us, length us, event | category | flops | bytes accessed | tf_op | source)
XLA Modules:
  0.0 261.8 jit_solution(14610194158688210043)
XLA Ops:
  0.6 5.0 %collective-permute-start.3 = (f32[512,768]{1,0:T(8,128)}, f32[512,768]{1,0:T(8,128)S(1)}, u32[]{:S(2)}, u32[]{:S(2)}) collective-permute-start(f32[512,768]{1,0:T(8,128)} %bitcast.19), channel_id=1, source_target_pairs={{16,17},{17,18},{18,19},{0,1},{1,2},{20,21},{21,22},{22,23},{4,5},... | collective-permute-start | bytes 4718600 | tf_op jit(solution)/shard_map/ppermute | solution.py:302
  6.5 1.9 dynamic-slice_bitcast_fusion
  8.3 1.5 collective-permute-start
  9.8 1.5 collective-permute-start.1
  12.5 1.3 dynamic_slice.16
  14.6 2.2 copy-done
  16.8 1.4 copy-done.1
  18.2 1.3 pack.1
  21.0 0.9 constant_dynamic-update-slice_fusion.2
  22.0 0.9 constant_dynamic-update-slice_fusion.1
  22.9 0.9 constant_dynamic-update-slice_fusion.refs_1_
  23.8 9.3 %collective-permute-start.4 = (f32[192,768]{1,0:T(8,128)S(1)}, f32[192,768]{1,0:T(8,128)S(1)}, u32[]{:S(2)}, u32[]{:S(2)}) collective-permute-start(f32[192,768]{1,0:T(8,128)S(1)} %constant_dynamic-update-slice_fusion.refs_1_), channel_id=1, source_target_pairs={{16,17},{17,18},{18,19},{0,1},{1,2},{20,21},{21,22},{22,23},{4,5},... | collective-permute-start | bytes 1769480 | tf_op jit(solution)/shard_map/ppermute | solution.py:302
  33.1 7.6 %collective-permute-done.3.refs_2_ = f32[512,768]{1,0:T(8,128)S(1)} collective-permute-done((f32[512,768]{1,0:T(8,128)}, f32[512,768]{1,0:T(8,128)S(1)}, u32[]{:S(2)}, u32[]{:S(2)}) %collective-permute-start.3) | collective-permute-done | bytes 1572896 | tf_op jit(solution)/shard_map/ppermute | solution.py:302
  41.8 10.2 %collective-permute-done.4.refs_3_ = f32[192,768]{1,0:T(8,128)S(1)} collective-permute-done((f32[192,768]{1,0:T(8,128)S(1)}, f32[192,768]{1,0:T(8,128)S(1)}, u32[]{:S(2)}, u32[]{:S(2)}) %collective-permute-start.4) | collective-permute-done | bytes 589856 | tf_op jit(solution)/shard_map/ppermute | solution.py:302
  53.5 1.2 copy-done.16
  54.7 1.2 copy-done.17
  55.8 0.8 collective-permute-start.10
  56.6 0.8 collective-permute-start.9
  58.2 10.2 %collective-permute-start.12 = (f32[2816,128]{1,0:T(8,128)S(1)}, f32[2816,128]{1,0:T(8,128)S(1)}, u32[]{:S(2)}, u32[]{:S(2)}) collective-permute-start(f32[2816,128]{1,0:T(8,128)S(1)} %get-tuple-element.52), channel_id=1, source_target_pairs={{0,1},{3,2},{4,5},{7,6},{8,9},{11,10},{12,13},{15,14}} | collective-permute-start | bytes 4325384 | tf_op jit(solution)/shard_map/ppermute | solution.py:354
  68.4 1.0 broadcast_select_fusion
  69.8 1.0 broadcast_select_fusion.1
  71.1 1.1 copy-done.19
  72.2 12.5 %collective-permute-done.12.refs_10_ = f32[2816,128]{1,0:T(8,128)S(1)} collective-permute-done((f32[2816,128]{1,0:T(8,128)S(1)}, f32[2816,128]{1,0:T(8,128)S(1)}, u32[]{:S(2)}, u32[]{:S(2)}) %collective-permute-start.12) | collective-permute-done | bytes 1441824 | tf_op jit(solution)/shard_map/ppermute | solution.py:354
  85.6 2.1 collective-permute-start.14
  87.6 21.0 %collective-permute-start.15 = (f32[2816,128]{1,0:T(8,128)S(1)}, f32[2816,128]{1,0:T(8,128)}, u32[]{:S(2)}, u32[]{:S(2)}) collective-permute-start(f32[2816,128]{1,0:T(8,128)S(1)} %get-tuple-element.55), channel_id=1, source_target_pairs={{0,5},{3,6},{4,1},{7,2},{8,13},{11,14},{12,9},{15,10}} | collective-permute-start | bytes 4325384 | tf_op jit(solution)/shard_map/ppermute | solution.py:354
  108.6 2.5 collective-permute-start.16
  111.1 2.4 collective-permute-start.17
  113.6 1.4 copy-done.15
  114.9 3.2 %first_block.1 = (f32[512,768]{1,0:T(8,128)}, f32[512,768]{1,0:T(8,128)}, f32[512,768]{1,0:T(8,128)}, f32[512,768]{1,0:T(8,128)}, f32[512,768]{1,0:T(8,128)}, /*...) custom-call(s32[4]{0:T(128)} %copy-done.2, f32[512,768]{1,0:T(8,128)} %bitcast.21, f32[192,768]{1,0:T(8,128)} %copy-done.12, ...), custom_call_target="tpu_custom_call" | custom-call | flops 13287555072 | bytes 31457280 | tf_op jit(solution)/shard_map/first_block/pallas_call | solution.py:253
  118.2 5.9 %collective-permute-done.15.refs_11_ = f32[2816,128]{1,0:T(8,128)} collective-permute-done((f32[2816,128]{1,0:T(8,128)S(1)}, f32[2816,128]{1,0:T(8,128)}, u32[]{:S(2)}, u32[]{:S(2)}) %collective-permute-start.15) | collective-permute-done | bytes 1441824 | tf_op jit(solution)/shard_map/ppermute | solution.py:354
  124.0 15.4 %collective-permute-done.16.refs_12_ = f32[2816,128]{1,0:T(8,128)} collective-permute-done((f32[2816,128]{1,0:T(8,128)S(1)}, f32[2816,128]{1,0:T(8,128)}, u32[]{:S(2)}, u32[]{:S(2)}) %collective-permute-start.16) | collective-permute-done | bytes 1441824 | tf_op jit(solution)/shard_map/ppermute | solution.py:354
  139.5 15.4 %collective-permute-done.17.refs_13_ = f32[2816,128]{1,0:T(8,128)} collective-permute-done((f32[2816,128]{1,0:T(8,128)S(1)}, f32[2816,128]{1,0:T(8,128)}, u32[]{:S(2)}, u32[]{:S(2)}) %collective-permute-start.17) | collective-permute-done | bytes 1441824 | tf_op jit(solution)/shard_map/ppermute | solution.py:354
  154.9 1.8 second_block.1
  157.5 1.0 collective-permute-start.18
  158.5 1.7 add.57
  161.3 0.9 collective-permute-start.19
  162.7 1.4 collective-permute-start.23
  164.1 1.3 add.56
  165.5 1.8 collective-permute-start.20
  169.3 1.5 collective-permute-start.24
  170.7 2.2 collective-permute-done.24
  172.9 1.5 collective-permute-start.25
  174.4 2.0 collective-permute-done.25
  176.4 72.6 %collective-permute-start.26 = (f32[32]{0:T(128)S(1)}, f32[32]{0:T(128)S(1)}, u32[]{:S(2)}, u32[]{:S(2)}) collective-permute-start(f32[32]{0:T(128)S(1)} %fusion.1), channel_id=1, source_target_pairs={{0,1},{1,0},{2,3},{3,2},{4,5},{5,4},{6,7},{7,6},{8,9},{9,8},{10,11... | collective-permute-start | bytes 392 | tf_op jit(solution)/shard_map/ppermute | solution.py:419
  249.0 2.8 %collective-permute-done.26 = f32[32]{0:T(128)S(1)} collective-permute-done((f32[32]{0:T(128)S(1)}, f32[32]{0:T(128)S(1)}, u32[]{:S(2)}, u32[]{:S(2)}) %collective-permute-start.26) | collective-permute-done | bytes 160 | tf_op jit(solution)/shard_map/ppermute | solution.py:419
  251.8 4.6 %collective-permute-start.27 = (f32[32]{0:T(128)S(1)}, f32[32]{0:T(128)S(1)}, u32[]{:S(2)}, u32[]{:S(2)}) collective-permute-start(f32[32]{0:T(128)S(1)} %add.64), channel_id=1, source_target_pairs={{0,2},{1,3},{2,0},{3,1},{4,6},{5,7},{6,4},{7,5},{8,10},{9,11},{10,... | collective-permute-start | bytes 392 | tf_op jit(solution)/shard_map/ppermute | solution.py:419
  256.4 1.5 collective-permute-done.27
  258.5 3.3 %add_bitcast_fusion = f32[1,1,512,768]{3,2,1,0:T(8,128)} fusion(f32[512,768]{1,0:T(8,128)} %get-tuple-element.65, f32[512,768]{1,0:T(8,128)} %collective-permute-done.20, f32[512,768]{1,0:T(8,128)S(1)} %collective-permute-done.23), kind=kLoop, calls=%fused_computation | loop fusion | flops 786432 | bytes 6291456 | tf_op jit(solution)/shard_map/broadcast_in_dim | solution.py:421
  (75 shorter events, 11.1 us)
Async XLA Ops:
  0.6 40.0 %collective-permute-start.3 = (f32[512,768]{1,0:T(8,128)}, f32[512,768]{1,0:T(8,128)S(1)}, u32[]{:S(2)}, u32[]{:S(2)}) collective-permute-start(f32[512,768]{1,0:T(8,128)} %bitcast.19), channel_id=1, source_target_pairs={{16,17},{17,18},{18,19},{0,1},{1,2},{20,21},{21,22},{22,23},{4,5},... | collective-permute-start | bytes 4718600 | tf_op jit(solution)/shard_map/ppermute | solution.py:302
  5.7 46.4 %collective-permute-start.5 = (f32[512,768]{1,0:T(8,128)}, f32[512,768]{1,0:T(8,128)S(1)}, u32[]{:S(2)}, u32[]{:S(2)}) collective-permute-start(f32[512,768]{1,0:T(8,128)} %bitcast.20), channel_id=1, source_target_pairs={{19,18},{18,17},{17,16},{3,2},{2,1},{23,22},{22,21},{21,20},{7,6},... | collective-permute-start | bytes 4718600 | tf_op jit(solution)/shard_map/ppermute | solution.py:302
  8.3 11.1 %collective-permute-start = (f32[48,768]{1,0:T(8,128)}, f32[48,768]{1,0:T(8,128)}, u32[]{:S(2)}, u32[]{:S(2)}) collective-permute-start(f32[48,768]{1,0:T(8,128)} %get-tuple-element.75), channel_id=1, source_target_pairs={{0,4},{1,5},{2,6},{3,7},{4,0},{5,1},{6,2},{7,3},{8,12},{9,13},{10,... | collective-permute-start | bytes 442376 | tf_op jit(solution)/shard_map/ppermute | solution.py:354
  9.8 9.7 %collective-permute-start.1 = (f32[48,768]{1,0:T(8,128)}, f32[48,768]{1,0:T(8,128)}, u32[]{:S(2)}, u32[]{:S(2)}) collective-permute-start(f32[48,768]{1,0:T(8,128)} %get-tuple-element.77), channel_id=1, source_target_pairs={{0,8},{1,9},{2,10},{3,11},{4,12},{5,13},{6,14},{7,15},{8,0},{9,1},... | collective-permute-start | bytes 442376 | tf_op jit(solution)/shard_map/ppermute | solution.py:354
  11.3 8.2 %collective-permute-start.2 = (f32[48,768]{1,0:T(8,128)S(1)}, f32[48,768]{1,0:T(8,128)}, u32[]{:S(2)}, u32[]{:S(2)}) collective-permute-start(f32[48,768]{1,0:T(8,128)S(1)} %get-tuple-element.74), channel_id=1, source_target_pairs={{0,12},{1,13},{2,14},{3,15},{4,8},{5,9},{6,10},{7,11},{8,4},{9,5},... | collective-permute-start | bytes 442376 | tf_op jit(solution)/shard_map/ppermute | solution.py:354
  14.6 2.2 copy-start
  16.8 1.4 copy-start.1
  18.2 1.3 copy-start.2
  19.5 34.0 %collective-permute-start.7 = (f32[2816,128]{1,0:T(8,128)S(1)}, f32[2816,128]{1,0:T(8,128)S(1)}, u32[]{:S(2)}, u32[]{:S(2)}) collective-permute-start(f32[2816,128]{1,0:T(8,128)S(1)} %get-tuple-element.55), channel_id=1, source_target_pairs={{1,5},{2,6},{5,1},{6,2},{9,13},{10,14},{13,9},{14,10},{16,20},{17,... | collective-permute-start | bytes 4325384 | tf_op jit(solution)/shard_map/ppermute | solution.py:354
  20.3 33.2 %collective-permute-start.8 = (f32[2816,128]{1,0:T(8,128)S(1)}, f32[2816,128]{1,0:T(8,128)S(1)}, u32[]{:S(2)}, u32[]{:S(2)}) collective-permute-start(f32[2816,128]{1,0:T(8,128)S(1)} %get-tuple-element.56), channel_id=1, source_target_pairs={{1,9},{2,10},{5,13},{6,14},{9,1},{10,2},{13,5},{14,6},{16,24},{17,... | collective-permute-start | bytes 4325384 | tf_op jit(solution)/shard_map/ppermute | solution.py:354
  23.8 17.7 %copy-start.12 = (f32[192,768]{1,0:T(8,128)}, f32[192,768]{1,0:T(8,128)S(1)}, u32[]{:S(2)}) copy-start(f32[192,768]{1,0:T(8,128)S(1)} %constant_dynamic-update-slice_fusion.refs_1_) | copy-start | bytes 1769476
  23.8 28.2 %collective-permute-start.4 = (f32[192,768]{1,0:T(8,128)S(1)}, f32[192,768]{1,0:T(8,128)S(1)}, u32[]{:S(2)}, u32[]{:S(2)}) collective-permute-start(f32[192,768]{1,0:T(8,128)S(1)} %constant_dynamic-update-slice_fusion.refs_1_), channel_id=1, source_target_pairs={{16,17},{17,18},{18,19},{0,1},{1,2},{20,21},{21,22},{22,23},{4,5},... | collective-permute-start | bytes 1769480 | tf_op jit(solution)/shard_map/ppermute | solution.py:302
  40.7 1.1 copy-start.5
  40.7 12.7 %collective-permute-start.6 = (f32[192,768]{1,0:T(8,128)S(1)}, f32[192,768]{1,0:T(8,128)S(1)}, u32[]{:S(2)}, u32[]{:S(2)}) collective-permute-start(f32[192,768]{1,0:T(8,128)S(1)} %constant_dynamic-update-slice_fusion.refs_1_), channel_id=1, source_target_pairs={{19,18},{18,17},{17,16},{3,2},{2,1},{23,22},{22,21},{21,20},{7,6},... | collective-permute-start | bytes 1769480 | tf_op jit(solution)/shard_map/ppermute | solution.py:302
  52.1 0.9 copy-start.10
  52.1 1.3 copy-start.6
  53.4 14.9 %copy-start.11 = (f32[192,768]{1,0:T(8,128)}, f32[192,768]{1,0:T(8,128)S(1)}, u32[]{:S(2)}) copy-start(f32[192,768]{1,0:T(8,128)S(1)} %collective-permute-done.6.refs_5_) | copy-start | bytes 1769476
  53.5 1.2 copy-start.16
  54.7 1.2 copy-start.17
  55.8 12.5 %collective-permute-start.10 = (f32[704,768]{1,0:T(8,128)S(1)}, f32[704,768]{1,0:T(8,128)S(1)}, u32[]{:S(2)}, u32[]{:S(2)}) collective-permute-start(f32[704,768]{1,0:T(8,128)S(1)} %constant_dynamic-update-slice_fusion.6), channel_id=1, source_target_pairs={{18,17},{17,16},{22,21},{21,20},{26,25},{25,24},{30,29},{29,28}} | collective-permute-start | bytes 6488072 | tf_op jit(solution)/shard_map/ppermute | solution.py:302
  56.6 13.1 %collective-permute-start.9 = (f32[704,768]{1,0:T(8,128)S(1)}, f32[704,768]{1,0:T(8,128)S(1)}, u32[]{:S(2)}, u32[]{:S(2)}) collective-permute-start(f32[704,768]{1,0:T(8,128)S(1)} %constant_dynamic-update-slice_fusion.4), channel_id=1, source_target_pairs={{17,18},{18,19},{21,22},{22,23},{25,26},{26,27},{29,30},{30,31}} | collective-permute-start | bytes 6488072 | tf_op jit(solution)/shard_map/ppermute | solution.py:302
  57.4 13.7 %collective-permute-start.11 = (f32[2816,128]{1,0:T(8,128)S(1)}, f32[2816,128]{1,0:T(8,128)S(1)}, u32[]{:S(2)}, u32[]{:S(2)}) collective-permute-start(f32[2816,128]{1,0:T(8,128)S(1)} %get-tuple-element.57), channel_id=1, source_target_pairs={{1,13},{2,14},{5,9},{6,10},{9,5},{10,6},{13,1},{14,2},{16,28},{17,... | collective-permute-start | bytes 4325384 | tf_op jit(solution)/shard_map/ppermute | solution.py:354
  58.2 26.6 %collective-permute-start.12 = (f32[2816,128]{1,0:T(8,128)S(1)}, f32[2816,128]{1,0:T(8,128)S(1)}, u32[]{:S(2)}, u32[]{:S(2)}) collective-permute-start(f32[2816,128]{1,0:T(8,128)S(1)} %get-tuple-element.52), channel_id=1, source_target_pairs={{0,1},{3,2},{4,5},{7,6},{8,9},{11,10},{12,13},{15,14}} | collective-permute-start | bytes 4325384 | tf_op jit(solution)/shard_map/ppermute | solution.py:354
  68.4 1.4 copy-start.3
  69.8 1.4 copy-start.4
  71.1 1.1 copy-start.19
  84.8 33.4 %copy-start.18 = (f32[2816,128]{1,0:T(8,128)}, f32[2816,128]{1,0:T(8,128)S(1)}, u32[]{:S(2)}) copy-start(f32[2816,128]{1,0:T(8,128)S(1)} %collective-permute-done.12.refs_10_) | copy-start | bytes 4325380
  84.8 28.8 %collective-permute-start.13 = (f32[704,768]{1,0:T(8,128)S(1)}, f32[704,768]{1,0:T(8,128)S(1)}, u32[]{:S(2)}, u32[]{:S(2)}) collective-permute-start(f32[704,768]{1,0:T(8,128)S(1)} %broadcast_select_fusion.1), channel_id=1, source_target_pairs={{18,19},{1,2},{22,23},{5,6},{26,27},{9,10},{30,31},{13,14}} | collective-permute-start | bytes 6488072 | tf_op jit(solution)/shard_map/ppermute | solution.py:302
  85.6 28.0 %collective-permute-start.14 = (f32[704,768]{1,0:T(8,128)S(1)}, f32[704,768]{1,0:T(8,128)}, u32[]{:S(2)}, u32[]{:S(2)}) collective-permute-start(f32[704,768]{1,0:T(8,128)S(1)} %broadcast_select_fusion), channel_id=1, source_target_pairs={{17,16},{2,1},{21,20},{6,5},{25,24},{10,9},{29,28},{14,13}} | collective-permute-start | bytes 6488072 | tf_op jit(solution)/shard_map/ppermute | solution.py:302
  87.6 36.4 %collective-permute-start.15 = (f32[2816,128]{1,0:T(8,128)S(1)}, f32[2816,128]{1,0:T(8,128)}, u32[]{:S(2)}, u32[]{:S(2)}) collective-permute-start(f32[2816,128]{1,0:T(8,128)S(1)} %get-tuple-element.55), channel_id=1, source_target_pairs={{0,5},{3,6},{4,1},{7,2},{8,13},{11,14},{12,9},{15,10}} | collective-permute-start | bytes 4325384 | tf_op jit(solution)/shard_map/ppermute | solution.py:354
  108.6 30.9 %collective-permute-start.16 = (f32[2816,128]{1,0:T(8,128)S(1)}, f32[2816,128]{1,0:T(8,128)}, u32[]{:S(2)}, u32[]{:S(2)}) collective-permute-start(f32[2816,128]{1,0:T(8,128)S(1)} %get-tuple-element.56), channel_id=1, source_target_pairs={{0,9},{3,10},{4,13},{7,14},{8,1},{11,2},{12,5},{15,6}} | collective-permute-start | bytes 4325384 | tf_op jit(solution)/shard_map/ppermute | solution.py:354
  111.1 43.8 %collective-permute-start.17 = (f32[2816,128]{1,0:T(8,128)S(1)}, f32[2816,128]{1,0:T(8,128)}, u32[]{:S(2)}, u32[]{:S(2)}) collective-permute-start(f32[2816,128]{1,0:T(8,128)S(1)} %get-tuple-element.57), channel_id=1, source_target_pairs={{0,13},{3,14},{4,9},{7,10},{8,5},{11,6},{12,1},{15,2}} | collective-permute-start | bytes 4325384 | tf_op jit(solution)/shard_map/ppermute | solution.py:354
  113.5 1.4 copy-start.15
  156.7 1.8 collective-permute-start.21
  157.5 3.6 %collective-permute-start.18 = (f32[512,768]{1,0:T(8,128)}, f32[512,768]{1,0:T(8,128)S(1)}, u32[]{:S(2)}, u32[]{:S(2)}) collective-permute-start(f32[512,768]{1,0:T(8,128)} %get-tuple-element.68), channel_id=1, source_target_pairs={{16,17},{20,21},{24,25},{28,29}} | collective-permute-start | bytes 4718600 | tf_op jit(solution)/shard_map/ppermute | solution.py:302
  158.5 2.5 copy-start.9
  160.3 1.9 collective-permute-start.22
  161.1 1.4 copy-start.7
  161.3 2.8 %collective-permute-start.19 = (f32[512,768]{1,0:T(8,128)S(1)}, f32[512,768]{1,0:T(8,128)S(1)}, u32[]{:S(2)}, u32[]{:S(2)}) collective-permute-start(f32[512,768]{1,0:T(8,128)S(1)} %add.55), channel_id=1, source_target_pairs={{1,2},{16,17},{17,18},{5,6},{20,21},{21,22},{9,10},{24,25},{25,26}... | collective-permute-start | bytes 4718600 | tf_op jit(solution)/shard_map/ppermute | solution.py:302
  162.5 1.6 copy-start.8
  162.7 95.8 %collective-permute-start.23 = (f32[512,768]{1,0:T(8,128)S(1)}, f32[512,768]{1,0:T(8,128)S(1)}, u32[]{:S(2)}, u32[]{:S(2)}) collective-permute-start(f32[512,768]{1,0:T(8,128)S(1)} %add.58), channel_id=1, source_target_pairs={{2,1},{1,0},{19,18},{18,17},{17,16},{6,5},{5,4},{23,22},{22,21},{2... | collective-permute-start | bytes 4718600 | tf_op jit(solution)/shard_map/ppermute | solution.py:302
  164.1 3.8 %copy-start.13 = (f32[1,768]{1,0:T(1,128)S(1)}, f32[1,768]{1,0:T(1,128)}, u32[]{:S(2)}) copy-start(f32[1,768]{1,0:T(1,128)} %get-tuple-element.72) | copy-start | bytes 9220
  164.1 3.8 %copy-start.14 = (f32[1,768]{1,0:T(1,128)S(1)}, f32[1,768]{1,0:T(1,128)}, u32[]{:S(2)}) copy-start(f32[1,768]{1,0:T(1,128)} %get-tuple-element.73) | copy-start | bytes 9220
  165.5 93.0 %collective-permute-start.20 = (f32[512,768]{1,0:T(8,128)}, f32[512,768]{1,0:T(8,128)}, u32[]{:S(2)}, u32[]{:S(2)}) collective-permute-start(f32[512,768]{1,0:T(8,128)} %add.56), channel_id=1, source_target_pairs={{1,2},{2,3},{16,17},{17,18},{18,19},{5,6},{6,7},{20,21},{21,22},{2... | collective-permute-start | bytes 4718600 | tf_op jit(solution)/shard_map/ppermute | solution.py:302
  169.3 3.6 %collective-permute-start.24 = (f32[32]{0:T(128)S(1)}, f32[32]{0:T(128)S(1)}, u32[]{:S(2)}, u32[]{:S(2)}) collective-permute-start(f32[32]{0:T(128)S(1)} %compare_select_fusion), channel_id=1, source_target_pairs={{0,4},{4,0},{8,12},{12,8},{1,5},{5,1},{9,13},{13,9},{2,6},{6,2},{1... | collective-permute-start | bytes 392 | tf_op jit(solution)/shard_map/ppermute | solution.py:419
  172.9 3.5 %collective-permute-start.25 = (f32[32]{0:T(128)S(1)}, f32[32]{0:T(128)S(1)}, u32[]{:S(2)}, u32[]{:S(2)}) collective-permute-start(f32[32]{0:T(128)S(1)} %fusion), channel_id=1, source_target_pairs={{0,8},{4,12},{8,0},{12,4},{1,9},{5,13},{9,1},{13,5},{2,10},{6,14},... | collective-permute-start | bytes 392 | tf_op jit(solution)/shard_map/ppermute | solution.py:419
  176.4 75.4 %collective-permute-start.26 = (f32[32]{0:T(128)S(1)}, f32[32]{0:T(128)S(1)}, u32[]{:S(2)}, u32[]{:S(2)}) collective-permute-start(f32[32]{0:T(128)S(1)} %fusion.1), channel_id=1, source_target_pairs={{0,1},{1,0},{2,3},{3,2},{4,5},{5,4},{6,7},{7,6},{8,9},{9,8},{10,11... | collective-permute-start | bytes 392 | tf_op jit(solution)/shard_map/ppermute | solution.py:419
  251.8 6.2 %collective-permute-start.27 = (f32[32]{0:T(128)S(1)}, f32[32]{0:T(128)S(1)}, u32[]{:S(2)}, u32[]{:S(2)}) collective-permute-start(f32[32]{0:T(128)S(1)} %add.64), channel_id=1, source_target_pairs={{0,2},{1,3},{2,0},{3,1},{4,6},{5,7},{6,4},{7,5},{8,10},{9,11},{10,... | collective-permute-start | bytes 392 | tf_op jit(solution)/shard_map/ppermute | solution.py:419

commit v2 on v1

--- a/solution.py
+++ b/solution.py
@@ -70,6 +70,39 @@
     )(meta, outs, eigs)
 
 
+def join_kernel(refs_in, groups, *refs):
+    sources, outs, sems = refs[1 : 1 + refs_in], refs[1 + refs_in : -1], refs[-1]
+    copies = []
+    at = 0
+    for out, number in zip(outs, groups):
+        first = 0
+        for source in sources[at : at + number]:
+            height = source.shape[0]
+            copies.append(pltpu.make_async_copy(source, out.at[pl.ds(first, height), :], sems.at[len(copies)]))
+            first += height
+        at += number
+    for copy in copies:
+        copy.start()
+    for copy in copies:
+        copy.wait()
+
+
+def join(groups, after):
+    sources = [x for group in groups for x in group]
+    in_hbm = pl.BlockSpec(memory_space=pltpu.HBM)
+    shapes = [jax.ShapeDtypeStruct((sum(x.shape[0] for x in group), group[0].shape[1]), F32) for group in groups]
+    return pl.pallas_call(
+        functools.partial(join_kernel, len(sources), [len(group) for group in groups]),
+        out_shape=shapes,
+        in_specs=[in_hbm] * (1 + len(sources)),
+        out_specs=[pl.BlockSpec(memory_space=pltpu.VMEM)] * len(shapes),
+        scratch_shapes=[pltpu.SemaphoreType.DMA((len(sources),))],
+        cost_estimate=pl.CostEstimate(flops=0, bytes_accessed=8 * sum(x.size for x in sources), transcendentals=0),
+        compiler_params=pltpu.CompilerParams(vmem_limit_bytes=32 * 1024 * 1024),
+        name="join",
+    )(after, *sources)
+
+
 def block_kernel(planes, inner_job, second, n_own, n_piece, fused, meta, *refs):
     refs = list(refs)
 
@@ -79,8 +112,7 @@
 
     hops = planes - 1
     here_refs = take(2 if fused else 1)
-    near_up, near_down = take(2 if fused else 1), take(2 if fused else 1)
-    far_up, far_down = take(hops - 1), take(hops - 1)
+    up_refs, down_refs = take(hops), take(hops)
     own_refs, piece_refs = take(n_own), take(n_piece)
     in_refs = take(0 if fused else 1)
     earlier = take(2 * planes - 1) if second else None
@@ -115,10 +147,8 @@
         distance = abs(target - plane)
         if distance == 0:
             return here_refs
-        if distance == 1:
-            return near_up if target < plane else near_down
-        step = hops if inner_only else distance
-        ref = (far_up if target < plane else far_down)[step - 2]
+        step = hops if inner_only and distance > 1 else distance
+        ref = (up_refs if target < plane else down_refs)[step - 1]
         if not fused:
             return [ref]
         return [ref.at[pl.ds(0, rows), :], ref.at[pl.ds(rows, ref.shape[0] - rows), :]]
@@ -320,18 +350,15 @@
         mark = x[:8, :128] + y[:8, :128]
         return lax.ppermute(mark, ("layer", "matrix"), [(planes + m, m) for m in range(planes)])
 
-    def near(x):
-        return move(x, gather_pairs(1)), move(x, mirror(gather_pairs(1)))
-
-    def far(below, above, ties):
-        ups, downs = [below], [above]
-        for step in range(2, planes):
+    def gather(x, ties):
+        ups, downs = [x], [x]
+        for step in range(1, planes):
             up, down = ups[-1], downs[-1]
             before = list(ties.get(step, ()))
             if any(inward) and step == last:
                 before.append(token(up, down))
-                up = jnp.where(takes_over, below, up)
-                down = jnp.where(takes_over, above, down)
+                up = jnp.where(takes_over, ups[1], up)
+                down = jnp.where(takes_over, downs[1], down)
             (up, down), _ = lax.optimization_barrier(((up, down), before))
             ups.append(move(up, gather_pairs(step)))
             downs.append(move(down, mirror(gather_pairs(step))))
@@ -342,71 +369,41 @@
     fits = columns % 128 == 0 and width % columns == 0 and columns == heights
     fits = fits and basis_in.shape[1] % 8 == 0 and experts & (experts - 1) == 0
 
-    def index(l, e, m):
-        return (l * experts + e) * planes + m
-
-    def goes_over(l, m):
-        return inward[l] and m in (0, last)
-
-    def crossing(x, distance, chosen, turn=lambda m: m):
-        every = [(l, e, m) for l in range(layers) for e in range(experts) for m in range(planes)]
-        pairs = [(index(l, e, m), index(l, e ^ distance, turn(m))) for l, e, m in every if chosen(l, m)]
-        return lax.ppermute(x, ("layer", "expert", "matrix"), pairs)
-
+    def crossing(x, distance):
+        return lax.ppermute(x, "expert", [(e, e ^ distance) for e in range(experts)])
+
+    end_pairs = [pair for l in range(layers) if inward[l] for pair in ((l, 0, 1), (l, last, last - 1))]
     own = grads[0, 0]
-    own_up, own_down = near(own)
     if fits:
         parts = [
             lax.dynamic_index_in_dim(basis_in, lax.bitwise_xor(expert, distance), 0, keepdims=False)
             for distance in range(experts)
         ]
-        parts = [x if d == 0 else crossing(x, d, lambda l, m: True) for d, x in enumerate(parts)]
+        parts = [x if d == 0 else crossing(x, d) for d, x in enumerate(parts)]
         packed = pack(meta, basis_out, eigvals)
         parts, packed = lax.optimization_barrier((parts, packed))
-        pieces = [crossing(packed[d], d, lambda l, m: not goes_over(l, m)) for d in range(1, experts)]
-        over = []
-        if any(inward):
-            packed, _ = lax.optimization_barrier((packed, (own_up, own_down)))
-            over = [crossing(packed[d], d, goes_over, lambda m: 1 if m == 0 else last - 1) for d in range(experts)]
-        part = jnp.concatenate(parts)
-        part_up, part_down = near(part)
-        ties = {2: pieces[:-1], 3: [*pieces[-1:], *over[:1]]}
-        below, above = far(jnp.concatenate([own_up, part_up]), jnp.concatenate([own_down, part_down]), ties)
-        near_shards = [own, part, own_up, part_up, own_down, part_down]
+        pieces = [crossing(packed[d], d) for d in range(1, experts)]
+        over = [move(x, end_pairs) for x in (packed[0], *pieces)] if any(inward) else []
+        part, payload = join([parts, [own, *parts]], packed[-1])
+        below, above = gather(payload, {2: pieces[:-1], 3: [*pieces[-1:], *over[:2]]})
+        here_shards = [own, part]
         first_owns, first_pieces, inners = [basis_out, eigvals], pieces, []
     else:
         eig = lax.all_to_all(eigvals, "expert", split_axis=0, concat_axis=1, tiled=True)[0]
         out = lax.all_to_all(basis_out, "expert", split_axis=0, concat_axis=2, tiled=True)[0]
         inner = lax.all_gather(basis_in, "matrix", axis=1, tiled=True)
         inner = lax.all_to_all(inner, "expert", split_axis=0, concat_axis=0, tiled=True).reshape(width, width)
-        below, above = far(own_up, own_down, {})
-        near_shards = [own, own_up, own_down]
+        below, above = gather(own, {})
+        over = []
+        here_shards = [own]
         first_owns, first_pieces, inners = [out, eig], [], [inner]
 
-    shards_of_job = [*near_shards, *below, *above]
+    shards_of_job = [*here_shards, *below, *above]
     sums, energy = run_block(planes, block, any(inward), meta, shards_of_job, first_owns, first_pieces, inners)
     if any(inward):
-        second_owns, second_pieces = [], []
-        if fits:
-            second_pieces = over
-        else:
-            ends = [pair for l in range(layers) if inward[l] for pair in ((l, 0, 1), (l, last, last - 1))]
-            second_owns = [move(x, ends) for x in first_owns]
-        sums, more = run_block(
-            planes, block, True, meta, shards_of_job, second_owns, second_pieces, inners, sums
-        )
+        owns = [] if fits else [move(x, end_pairs) for x in first_owns]
+        sums, more = run_block(planes, block, True, meta, shards_of_job, owns, over, inners, sums)
         energy = energy + more
-
-    below, above = sums[1:planes], sums[planes:]
-
-    def spread(partials, turn):
-        moved = None
-        for step in range(1, planes):
-            partial = partials[last - step]
-            moved = move(partial if moved is None else partial + moved, turn(reduce_pairs(step)))
-        return moved
-
-    result = sums[0] + (spread(above, lambda pairs: pairs) + spread(below, mirror))
 
     value = jnp.sum(energy) / (depth * width)
     scores = jnp.where(jnp.arange(QUERIES, dtype=jnp.int32) == slot_query[0, 0], value, 0.0)
@@ -416,8 +413,22 @@
             continue
         distance = 1
         while distance < size:
-            scores = scores + lax.ppermute(scores, axis, [(i, i ^ distance) for i in range(size)])
-            distance *= 2
+            turns = [distance * turn for turn in (1, 2, 3) if distance * turn < size]
+            moved = [lax.ppermute(scores, axis, [(i, i ^ turn) for i in range(size)]) for turn in turns]
+            scores = sum(moved, scores)
+            distance *= 4
+
+    below, above = sums[1:planes], sums[planes:]
+
+    def spread(partials, turn):
+        moved = None
+        for step in range(1, planes):
+            partial = partials[last - step]
+            sent = partial if moved is None else partial + moved
+            moved = move(sent, turn(reduce_pairs(step)))
+        return moved
+
+    result = sums[0] + (spread(above, lambda pairs: pairs) + spread(below, mirror))
     return (result[None, None], scores)
 
 

time: 263 us -> 262 us (level)
  waiting for transfers between devices: 75.6 us -> 98.2 us
  starting transfers between devices: 149 us -> 133 us
  local copies, waits for them, and re-layouts: 17.3 us -> 8.93 us
    ppermute x14 -> x16, waiting for transfers between devices: 17.8 us -> 50.6 us  [move(): lax.ppermute(x, ('layer', 'matrix'), [(l * planes + a, l * planes + b) fo...]
    ppermute x14 -> x12, starting transfers between devices: 122 us -> 98.7 us  [the longest x6 88.6 us: shards(): lax.ppermute(scores, axis, [(i, i ^ turn) for i in range(size)])]
    ppermute x14 -> x12, waiting for transfers between devices: 57.8 us -> 47.6 us  [the longest x6 40.7 us: crossing(): lax.ppermute(x, 'expert', [(e, e ^ distance) for e in range(experts)])]
    ppermute x14 -> x16, starting transfers between devices: 26.9 us -> 34.2 us  [move(): lax.ppermute(x, ('layer', 'matrix'), [(l * planes + a, l * planes + b) fo...]
    unnamed x45 -> x42, local copies, waits for them, and re-layouts: 13.1 us -> 6.51 us
  transfers between devices with their start and end apart: 28 -> 28, of which waited for: 10 -> 12; matrix products, arithmetic and copies ran while one was open for 5% -> 3% of each run, Pallas kernels for 2% -> 2%
where the time goes in v2:
time: 262 us
  starting transfers between devices  133 us (51%)
  waiting for transfers between devices  98.2 us (37%)
  other arithmetic  9.88 us (4%)
  local copies, waits for them, and re-layouts  8.93 us (3%)
  Pallas kernels  7.96 us (3%)
  between operations  3.69 us (1%)
    ppermute x6, starting transfers between devices, shards(): lax.ppermute(scores, axis, [(i, i ^ turn) for i in range(size)])  88.6 us
    ppermute x16, waiting for transfers between devices, move(): lax.ppermute(x, ('layer', 'matrix'), [(l * planes + a, l * planes + b) fo...  50.6 us
    ppermute x6, waiting for transfers between devices, crossing(): lax.ppermute(x, 'expert', [(e, e ^ distance) for e in range(experts)])  40.7 us
    ppermute x16, starting transfers between devices, move(): lax.ppermute(x, ('layer', 'matrix'), [(l * planes + a, l * planes + b) fo...  34.2 us
    ppermute x6, starting transfers between devices, crossing(): lax.ppermute(x, 'expert', [(e, e ^ distance) for e in range(experts)])  10.1 us
    ppermute x6, waiting for transfers between devices, shards(): lax.ppermute(scores, axis, [(i, i ^ turn) for i in range(size)])  6.96 us
    unnamed x42, local copies, waits for them, and re-layouts  6.51 us
  transfers between devices with their start and end apart: 28, of which 12 were waited for; matrix products, arithmetic and copies ran while one was open for 3% of the time, Pallas kernels for 2%

profile of v2, /device:TPU:0, one launch (start us, length us, event | category | flops | bytes accessed | tf_op | source)
XLA Modules:
  0.0 261.6 jit_solution(1885211010590883890)
XLA Ops:
  0.6 1.2 dynamic-slice_bitcast_fusion
  1.8 3.0 %collective-permute-start = (f32[48,768]{1,0:T(8,128)S(1)}, f32[48,768]{1,0:T(8,128)S(1)}, u32[]{:S(2)}, u32[]{:S(2)}) collective-permute-start(f32[48,768]{1,0:T(8,128)S(1)} %get-tuple-element.75), channel_id=1, source_target_pairs={{0,4},{4,0},{8,12},{12,8},{1,5},{5,1},{9,13},{13,9},{2,6},{6,2},{1... | collective-permute-start | bytes 442376 | tf_op jit(solution)/shard_map/ppermute | solution.py:373
  4.8 1.5 collective-permute-start.1
  7.0 1.2 dynamic_slice.16
  9.0 2.2 copy-done
  11.2 1.4 copy-done.1
  12.6 1.3 pack.1
  14.0 1.7 join.1
  15.7 4.1 %collective-permute-start.3 = (f32[704,768]{1,0:T(8,128)S(1)}, f32[704,768]{1,0:T(8,128)S(1)}, u32[]{:S(2)}, u32[]{:S(2)}) collective-permute-start(f32[704,768]{1,0:T(8,128)S(1)} %get-tuple-element.50), channel_id=1, source_target_pairs={{16,17},{17,18},{18,19},{0,1},{1,2},{20,21},{21,22},{22,23},{4,5},... | collective-permute-start | bytes 6488072 | tf_op jit(solution)/shard_map/ppermute | solution.py:332
  19.8 0.8 collective-permute-start.4
  20.6 1.6 collective-permute-start.5
  22.2 1.5 collective-permute-start.6
  23.7 29.7 %collective-permute-done.5.refs_10_ = f32[2816,128]{1,0:T(8,128)S(1)} collective-permute-done((f32[2816,128]{1,0:T(8,128)S(1)}, f32[2816,128]{1,0:T(8,128)S(1)}, u32[]{:S(2)}, u32[]{:S(2)}) %collective-permute-start.5) | collective-permute-done | bytes 1441824 | tf_op jit(solution)/shard_map/ppermute | solution.py:373
  53.4 1.2 collective-permute-done.6.refs_11_
  54.6 10.5 %collective-permute-done.3.refs_2_ = f32[704,768]{1,0:T(8,128)S(1)} collective-permute-done((f32[704,768]{1,0:T(8,128)S(1)}, f32[704,768]{1,0:T(8,128)S(1)}, u32[]{:S(2)}, u32[]{:S(2)}) %collective-permute-start.3) | collective-permute-done | bytes 2162720 | tf_op jit(solution)/shard_map/ppermute | solution.py:332
  65.1 0.8 collective-permute-start.8
  65.9 0.8 collective-permute-start.7
  66.7 7.7 %collective-permute-start.10 = (f32[2816,128]{1,0:T(8,128)S(1)}, f32[2816,128]{1,0:T(8,128)S(1)}, u32[]{:S(2)}, u32[]{:S(2)}) collective-permute-start(f32[2816,128]{1,0:T(8,128)S(1)} %get-tuple-element.55), channel_id=1, source_target_pairs={{0,1},{3,2},{4,5},{7,6},{8,9},{11,10},{12,13},{15,14}} | collective-permute-start | bytes 4325384 | tf_op jit(solution)/shard_map/ppermute | solution.py:332
  74.4 2.5 collective-permute-start.9
  76.9 1.4 collective-permute-start.11
  78.3 0.9 broadcast_select_fusion
  79.3 0.9 broadcast_select_fusion.1
  80.7 10.1 %collective-permute-done.10.refs_8_ = f32[2816,128]{1,0:T(8,128)S(1)} collective-permute-done((f32[2816,128]{1,0:T(8,128)S(1)}, f32[2816,128]{1,0:T(8,128)S(1)}, u32[]{:S(2)}, u32[]{:S(2)}) %collective-permute-start.10) | collective-permute-done | bytes 1441824 | tf_op jit(solution)/shard_map/ppermute | solution.py:332
  90.8 9.8 %collective-permute-done.9.refs_12_ = f32[2816,128]{1,0:T(8,128)} collective-permute-done((f32[2816,128]{1,0:T(8,128)S(1)}, f32[2816,128]{1,0:T(8,128)}, u32[]{:S(2)}, u32[]{:S(2)}) %collective-permute-start.9) | collective-permute-done | bytes 1441824 | tf_op jit(solution)/shard_map/ppermute | solution.py:373
  100.6 5.7 %collective-permute-done.11.refs_9_ = f32[2816,128]{1,0:T(8,128)S(1)} collective-permute-done((f32[2816,128]{1,0:T(8,128)S(1)}, f32[2816,128]{1,0:T(8,128)S(1)}, u32[]{:S(2)}, u32[]{:S(2)}) %collective-permute-start.11) | collective-permute-done | bytes 1441824 | tf_op jit(solution)/shard_map/ppermute | solution.py:332
  106.3 0.8 collective-permute-start.12
  107.1 0.8 collective-permute-start.13
  107.9 8.0 %collective-permute-start.14 = (f32[2816,128]{1,0:T(8,128)S(1)}, f32[2816,128]{1,0:T(8,128)S(1)}, u32[]{:S(2)}, u32[]{:S(2)}) collective-permute-start(f32[2816,128]{1,0:T(8,128)S(1)} %collective-permute-done.6.refs_11_), channel_id=1, source_target_pairs={{0,1},{3,2},{4,5},{7,6},{8,9},{11,10},{12,13},{15,14}} | collective-permute-start | bytes 4325384 | tf_op jit(solution)/shard_map/ppermute | solution.py:332
  115.9 2.4 collective-permute-start.15
  118.3 1.4 copy-done.14
  120.4 3.2 %first_block.1 = (f32[512,768]{1,0:T(8,128)}, f32[512,768]{1,0:T(8,128)}, f32[512,768]{1,0:T(8,128)}, f32[512,768]{1,0:T(8,128)}, f32[512,768]{1,0:T(8,128)}, /*...) custom-call(s32[4]{0:T(128)} %copy-done.3, f32[512,768]{1,0:T(8,128)} %bitcast.18, f32[192,768]{1,0:T(8,128)} %copy-done.4, ...), custom_call_target="tpu_custom_call" | custom-call | flops 13287555072 | bytes 31457280 | tf_op jit(solution)/shard_map/first_block/pallas_call | solution.py:283
  123.6 8.7 %collective-permute-done.14.refs_10_ = f32[2816,128]{1,0:T(8,128)S(1)} collective-permute-done((f32[2816,128]{1,0:T(8,128)S(1)}, f32[2816,128]{1,0:T(8,128)S(1)}, u32[]{:S(2)}, u32[]{:S(2)}) %collective-permute-start.14) | collective-permute-done | bytes 1441824 | tf_op jit(solution)/shard_map/ppermute | solution.py:332
  132.3 15.6 %collective-permute-done.15.refs_11_ = f32[2816,128]{1,0:T(8,128)} collective-permute-done((f32[2816,128]{1,0:T(8,128)}, f32[2816,128]{1,0:T(8,128)}, u32[]{:S(2)}, u32[]{:S(2)}) %collective-permute-start.15) | collective-permute-done | bytes 1441824 | tf_op jit(solution)/shard_map/ppermute | solution.py:332
  147.8 1.8 second_block.1
  150.4 1.0 collective-permute-start.16
  151.4 1.7 add.63
  154.2 0.9 collective-permute-start.17
  155.6 1.4 collective-permute-start.21
  157.0 1.4 add.62
  158.4 1.8 collective-permute-start.18
  162.2 1.6 collective-permute-start.22
  163.7 1.5 collective-permute-start.23
  165.8 1.5 collective-permute-done.23
  167.3 2.4 collective-permute-done.24
  169.7 82.6 %collective-permute-start.25 = (f32[32]{0:T(128)S(1)}, f32[32]{0:T(128)S(1)}, u32[]{:S(2)}, u32[]{:S(2)}) collective-permute-start(f32[32]{0:T(128)S(1)} %add_add_fusion.1), channel_id=1, source_target_pairs={{0,1},{1,0},{2,3},{3,2},{4,5},{5,4},{6,7},{7,6},{8,9},{9,8},{10,11... | collective-permute-start | bytes 392 | tf_op jit(solution)/shard_map/ppermute | solution.py:417
  252.3 2.4 collective-permute-start.27
  254.7 3.0 %collective-permute-done.26 = f32[32]{0:T(128)S(1)} collective-permute-done((f32[32]{0:T(128)S(1)}, f32[32]{0:T(128)S(1)}, u32[]{:S(2)}, u32[]{:S(2)}) %collective-permute-start.26) | collective-permute-done | bytes 160 | tf_op jit(solution)/shard_map/ppermute | solution.py:417
  258.3 3.3 %add_bitcast_fusion = f32[1,1,512,768]{3,2,1,0:T(8,128)} fusion(f32[512,768]{1,0:T(8,128)} %get-tuple-element.65, f32[512,768]{1,0:T(8,128)} %collective-permute-done.18, f32[512,768]{1,0:T(8,128)S(1)} %collective-permute-done.21), kind=kLoop, calls=%fused_computation | loop fusion | flops 786432 | bytes 6291456 | tf_op jit(solution)/shard_map/broadcast_in_dim | solution.py:432
  (68 shorter events, 5.2 us)
Async XLA Ops:
  1.8 12.1 %collective-permute-start = (f32[48,768]{1,0:T(8,128)S(1)}, f32[48,768]{1,0:T(8,128)S(1)}, u32[]{:S(2)}, u32[]{:S(2)}) collective-permute-start(f32[48,768]{1,0:T(8,128)S(1)} %get-tuple-element.75), channel_id=1, source_target_pairs={{0,4},{4,0},{8,12},{12,8},{1,5},{5,1},{9,13},{13,9},{2,6},{6,2},{1... | collective-permute-start | bytes 442376 | tf_op jit(solution)/shard_map/ppermute | solution.py:373
  4.8 9.1 %collective-permute-start.1 = (f32[48,768]{1,0:T(8,128)S(1)}, f32[48,768]{1,0:T(8,128)S(1)}, u32[]{:S(2)}, u32[]{:S(2)}) collective-permute-start(f32[48,768]{1,0:T(8,128)S(1)} %get-tuple-element.77), channel_id=1, source_target_pairs={{0,8},{4,12},{8,0},{12,4},{1,9},{5,13},{9,1},{13,5},{2,10},{6,14},... | collective-permute-start | bytes 442376 | tf_op jit(solution)/shard_map/ppermute | solution.py:373
  6.3 7.6 %collective-permute-start.2 = (f32[48,768]{1,0:T(8,128)S(1)}, f32[48,768]{1,0:T(8,128)S(1)}, u32[]{:S(2)}, u32[]{:S(2)}) collective-permute-start(f32[48,768]{1,0:T(8,128)S(1)} %get-tuple-element.74), channel_id=1, source_target_pairs={{0,12},{4,8},{8,4},{12,0},{1,13},{5,9},{9,5},{13,1},{2,14},{6,10},... | collective-permute-start | bytes 442376 | tf_op jit(solution)/shard_map/ppermute | solution.py:373
  9.0 2.2 copy-start
  11.2 1.4 copy-start.1
  12.6 1.4 copy-start.2
  15.7 63.6 %copy-start.4 = (f32[192,768]{1,0:T(8,128)}, f32[192,768]{1,0:T(8,128)S(1)}, u32[]{:S(2)}) copy-start(f32[192,768]{1,0:T(8,128)S(1)} %get-tuple-element.47.refs_1_) | copy-start | bytes 1769476
  15.7 49.4 %collective-permute-start.3 = (f32[704,768]{1,0:T(8,128)S(1)}, f32[704,768]{1,0:T(8,128)S(1)}, u32[]{:S(2)}, u32[]{:S(2)}) collective-permute-start(f32[704,768]{1,0:T(8,128)S(1)} %get-tuple-element.50), channel_id=1, source_target_pairs={{16,17},{17,18},{18,19},{0,1},{1,2},{20,21},{21,22},{22,23},{4,5},... | collective-permute-start | bytes 6488072 | tf_op jit(solution)/shard_map/ppermute | solution.py:332
  19.8 45.3 %collective-permute-start.4 = (f32[704,768]{1,0:T(8,128)S(1)}, f32[704,768]{1,0:T(8,128)S(1)}, u32[]{:S(2)}, u32[]{:S(2)}) collective-permute-start(f32[704,768]{1,0:T(8,128)S(1)} %get-tuple-element.50), channel_id=1, source_target_pairs={{19,18},{18,17},{17,16},{3,2},{2,1},{23,22},{22,21},{21,20},{7,6},... | collective-permute-start | bytes 6488072 | tf_op jit(solution)/shard_map/ppermute | solution.py:332
  20.6 32.8 %collective-permute-start.5 = (f32[2816,128]{1,0:T(8,128)S(1)}, f32[2816,128]{1,0:T(8,128)S(1)}, u32[]{:S(2)}, u32[]{:S(2)}) collective-permute-start(f32[2816,128]{1,0:T(8,128)S(1)} %get-tuple-element.51), channel_id=1, source_target_pairs={{0,4},{4,0},{8,12},{12,8},{1,5},{5,1},{9,13},{13,9},{2,6},{6,2},{1... | collective-permute-start | bytes 4325384 | tf_op jit(solution)/shard_map/ppermute | solution.py:373
  22.2 32.4 %collective-permute-start.6 = (f32[2816,128]{1,0:T(8,128)S(1)}, f32[2816,128]{1,0:T(8,128)S(1)}, u32[]{:S(2)}, u32[]{:S(2)}) collective-permute-start(f32[2816,128]{1,0:T(8,128)S(1)} %get-tuple-element.52), channel_id=1, source_target_pairs={{0,8},{4,12},{8,0},{12,4},{1,9},{5,13},{9,1},{13,5},{2,10},{6,14},... | collective-permute-start | bytes 4325384 | tf_op jit(solution)/shard_map/ppermute | solution.py:373
  53.4 25.9 %copy-start.16 = (f32[2816,128]{1,0:T(8,128)}, f32[2816,128]{1,0:T(8,128)S(1)}, u32[]{:S(2)}) copy-start(f32[2816,128]{1,0:T(8,128)S(1)} %collective-permute-done.5.refs_10_) | copy-start | bytes 4325380
  54.6 53.3 %copy-start.17 = (f32[2816,128]{1,0:T(8,128)}, f32[2816,128]{1,0:T(8,128)S(1)}, u32[]{:S(2)}) copy-start(f32[2816,128]{1,0:T(8,128)S(1)} %collective-permute-done.6.refs_11_) | copy-start | bytes 4325380
  65.1 14.2 %copy-start.5 = (f32[704,768]{1,0:T(8,128)}, f32[704,768]{1,0:T(8,128)S(1)}, u32[]{:S(2)}) copy-start(f32[704,768]{1,0:T(8,128)S(1)} %collective-permute-done.3.refs_2_) | copy-start | bytes 6488068
  65.1 14.2 %copy-start.6 = (f32[704,768]{1,0:T(8,128)}, f32[704,768]{1,0:T(8,128)S(1)}, u32[]{:S(2)}) copy-start(f32[704,768]{1,0:T(8,128)S(1)} %collective-permute-done.4.refs_5_) | copy-start | bytes 6488068
  65.1 13.2 %collective-permute-start.8 = (f32[704,768]{1,0:T(8,128)S(1)}, f32[704,768]{1,0:T(8,128)S(1)}, u32[]{:S(2)}, u32[]{:S(2)}) collective-permute-start(f32[704,768]{1,0:T(8,128)S(1)} %collective-permute-done.4.refs_5_), channel_id=1, source_target_pairs={{18,17},{17,16},{22,21},{21,20},{26,25},{25,24},{30,29},{29,28}} | collective-permute-start | bytes 6488072 | tf_op jit(solution)/shard_map/ppermute | solution.py:332
  65.9 13.4 %collective-permute-start.7 = (f32[704,768]{1,0:T(8,128)S(1)}, f32[704,768]{1,0:T(8,128)S(1)}, u32[]{:S(2)}, u32[]{:S(2)}) collective-permute-start(f32[704,768]{1,0:T(8,128)S(1)} %collective-permute-done.3.refs_2_), channel_id=1, source_target_pairs={{17,18},{18,19},{21,22},{22,23},{25,26},{26,27},{29,30},{30,31}} | collective-permute-start | bytes 6488072 | tf_op jit(solution)/shard_map/ppermute | solution.py:332
  66.7 24.1 %collective-permute-start.10 = (f32[2816,128]{1,0:T(8,128)S(1)}, f32[2816,128]{1,0:T(8,128)S(1)}, u32[]{:S(2)}, u32[]{:S(2)}) collective-permute-start(f32[2816,128]{1,0:T(8,128)S(1)} %get-tuple-element.55), channel_id=1, source_target_pairs={{0,1},{3,2},{4,5},{7,6},{8,9},{11,10},{12,13},{15,14}} | collective-permute-start | bytes 4325384 | tf_op jit(solution)/shard_map/ppermute | solution.py:332
  74.4 26.2 %collective-permute-start.9 = (f32[2816,128]{1,0:T(8,128)S(1)}, f32[2816,128]{1,0:T(8,128)}, u32[]{:S(2)}, u32[]{:S(2)}) collective-permute-start(f32[2816,128]{1,0:T(8,128)S(1)} %get-tuple-element.42.refs_0_), channel_id=1, source_target_pairs={{0,12},{4,8},{8,4},{12,0},{1,13},{5,9},{9,5},{13,1},{2,14},{6,10},... | collective-permute-start | bytes 4325384 | tf_op jit(solution)/shard_map/ppermute | solution.py:373
  76.9 29.4 %collective-permute-start.11 = (f32[2816,128]{1,0:T(8,128)S(1)}, f32[2816,128]{1,0:T(8,128)S(1)}, u32[]{:S(2)}, u32[]{:S(2)}) collective-permute-start(f32[2816,128]{1,0:T(8,128)S(1)} %collective-permute-done.5.refs_10_), channel_id=1, source_target_pairs={{0,1},{3,2},{4,5},{7,6},{8,9},{11,10},{12,13},{15,14}} | collective-permute-start | bytes 4325384 | tf_op jit(solution)/shard_map/ppermute | solution.py:332
  78.3 2.0 copy-start.7
  79.3 1.4 copy-start.8
  90.8 27.5 %copy-start.18 = (f32[2816,128]{1,0:T(8,128)}, f32[2816,128]{1,0:T(8,128)S(1)}, u32[]{:S(2)}) copy-start(f32[2816,128]{1,0:T(8,128)S(1)} %collective-permute-done.10.refs_8_) | copy-start | bytes 4325380
  106.3 12.0 %copy-start.19 = (f32[2816,128]{1,0:T(8,128)}, f32[2816,128]{1,0:T(8,128)S(1)}, u32[]{:S(2)}) copy-start(f32[2816,128]{1,0:T(8,128)S(1)} %collective-permute-done.11.refs_9_) | copy-start | bytes 4325380
  106.3 12.0 %collective-permute-start.12 = (f32[704,768]{1,0:T(8,128)S(1)}, f32[704,768]{1,0:T(8,128)S(1)}, u32[]{:S(2)}, u32[]{:S(2)}) collective-permute-start(f32[704,768]{1,0:T(8,128)S(1)} %broadcast_select_fusion.1), channel_id=1, source_target_pairs={{18,19},{1,2},{22,23},{5,6},{26,27},{9,10},{30,31},{13,14}} | collective-permute-start | bytes 6488072 | tf_op jit(solution)/shard_map/ppermute | solution.py:332
  107.1 11.2 %collective-permute-start.13 = (f32[704,768]{1,0:T(8,128)S(1)}, f32[704,768]{1,0:T(8,128)S(1)}, u32[]{:S(2)}, u32[]{:S(2)}) collective-permute-start(f32[704,768]{1,0:T(8,128)S(1)} %broadcast_select_fusion), channel_id=1, source_target_pairs={{17,16},{2,1},{21,20},{6,5},{25,24},{10,9},{29,28},{14,13}} | collective-permute-start | bytes 6488072 | tf_op jit(solution)/shard_map/ppermute | solution.py:332
  107.9 24.4 %collective-permute-start.14 = (f32[2816,128]{1,0:T(8,128)S(1)}, f32[2816,128]{1,0:T(8,128)S(1)}, u32[]{:S(2)}, u32[]{:S(2)}) collective-permute-start(f32[2816,128]{1,0:T(8,128)S(1)} %collective-permute-done.6.refs_11_), channel_id=1, source_target_pairs={{0,1},{3,2},{4,5},{7,6},{8,9},{11,10},{12,13},{15,14}} | collective-permute-start | bytes 4325384 | tf_op jit(solution)/shard_map/ppermute | solution.py:332
  115.9 32.0 %collective-permute-start.15 = (f32[2816,128]{1,0:T(8,128)}, f32[2816,128]{1,0:T(8,128)}, u32[]{:S(2)}, u32[]{:S(2)}) collective-permute-start(f32[2816,128]{1,0:T(8,128)} %collective-permute-done.9.refs_12_), channel_id=1, source_target_pairs={{0,1},{3,2},{4,5},{7,6},{8,9},{11,10},{12,13},{15,14}} | collective-permute-start | bytes 4325384 | tf_op jit(solution)/shard_map/ppermute | solution.py:332
  118.3 1.4 copy-start.14
  118.3 2.1 copy-start.15
  132.3 15.6 %copy-start.20 = (f32[2816,128]{1,0:T(8,128)}, f32[2816,128]{1,0:T(8,128)S(1)}, u32[]{:S(2)}) copy-start(f32[2816,128]{1,0:T(8,128)S(1)} %collective-permute-done.14.refs_10_) | copy-start | bytes 4325380
  149.6 1.8 collective-permute-start.19
  150.4 3.6 %collective-permute-start.16 = (f32[512,768]{1,0:T(8,128)}, f32[512,768]{1,0:T(8,128)S(1)}, u32[]{:S(2)}, u32[]{:S(2)}) collective-permute-start(f32[512,768]{1,0:T(8,128)} %get-tuple-element.68), channel_id=1, source_target_pairs={{16,17},{20,21},{24,25},{28,29}} | collective-permute-start | bytes 4718600 | tf_op jit(solution)/shard_map/ppermute | solution.py:332
  151.4 2.5 copy-start.11
  153.2 1.9 collective-permute-start.20
  154.0 1.4 copy-start.9
  154.2 2.8 %collective-permute-start.17 = (f32[512,768]{1,0:T(8,128)S(1)}, f32[512,768]{1,0:T(8,128)S(1)}, u32[]{:S(2)}, u32[]{:S(2)}) collective-permute-start(f32[512,768]{1,0:T(8,128)S(1)} %add.61), channel_id=1, source_target_pairs={{1,2},{16,17},{17,18},{5,6},{20,21},{21,22},{9,10},{24,25},{25,26}... | collective-permute-start | bytes 4718600 | tf_op jit(solution)/shard_map/ppermute | solution.py:332
  155.4 1.6 copy-start.10
  155.6 102.7 %collective-permute-start.21 = (f32[512,768]{1,0:T(8,128)S(1)}, f32[512,768]{1,0:T(8,128)S(1)}, u32[]{:S(2)}, u32[]{:S(2)}) collective-permute-start(f32[512,768]{1,0:T(8,128)S(1)} %add.64), channel_id=1, source_target_pairs={{2,1},{1,0},{19,18},{18,17},{17,16},{6,5},{5,4},{23,22},{22,21},{2... | collective-permute-start | bytes 4718600 | tf_op jit(solution)/shard_map/ppermute | solution.py:332
  157.0 3.8 %copy-start.12 = (f32[1,768]{1,0:T(1,128)S(1)}, f32[1,768]{1,0:T(1,128)}, u32[]{:S(2)}) copy-start(f32[1,768]{1,0:T(1,128)} %get-tuple-element.72) | copy-start | bytes 9220
  157.0 3.8 %copy-start.13 = (f32[1,768]{1,0:T(1,128)S(1)}, f32[1,768]{1,0:T(1,128)}, u32[]{:S(2)}) copy-start(f32[1,768]{1,0:T(1,128)} %get-tuple-element.73) | copy-start | bytes 9220
  158.4 99.9 %collective-permute-start.18 = (f32[512,768]{1,0:T(8,128)}, f32[512,768]{1,0:T(8,128)}, u32[]{:S(2)}, u32[]{:S(2)}) collective-permute-start(f32[512,768]{1,0:T(8,128)} %add.62), channel_id=1, source_target_pairs={{1,2},{2,3},{16,17},{17,18},{18,19},{5,6},{6,7},{20,21},{21,22},{2... | collective-permute-start | bytes 4718600 | tf_op jit(solution)/shard_map/ppermute | solution.py:332
  162.2 3.6 %collective-permute-start.22 = (f32[32]{0:T(128)S(1)}, f32[32]{0:T(128)S(1)}, u32[]{:S(2)}, u32[]{:S(2)}) collective-permute-start(f32[32]{0:T(128)S(1)} %compare_select_fusion), channel_id=1, source_target_pairs={{0,4},{4,0},{8,12},{12,8},{1,5},{5,1},{9,13},{13,9},{2,6},{6,2},{1... | collective-permute-start | bytes 392 | tf_op jit(solution)/shard_map/ppermute | solution.py:417
  163.7 3.5 %collective-permute-start.23 = (f32[32]{0:T(128)S(1)}, f32[32]{0:T(128)S(1)}, u32[]{:S(2)}, u32[]{:S(2)}) collective-permute-start(f32[32]{0:T(128)S(1)} %compare_select_fusion), channel_id=1, source_target_pairs={{0,8},{4,12},{8,0},{12,4},{1,9},{5,13},{9,1},{13,5},{2,10},{6,14},... | collective-permute-start | bytes 392 | tf_op jit(solution)/shard_map/ppermute | solution.py:417
  165.2 4.4 %collective-permute-start.24 = (f32[32]{0:T(128)S(1)}, f32[32]{0:T(128)S(1)}, u32[]{:S(2)}, u32[]{:S(2)}) collective-permute-start(f32[32]{0:T(128)S(1)} %compare_select_fusion), channel_id=1, source_target_pairs={{0,12},{4,8},{8,4},{12,0},{1,13},{5,9},{9,5},{13,1},{2,14},{6,10},... | collective-permute-start | bytes 392 | tf_op jit(solution)/shard_map/ppermute | solution.py:417
  169.7 85.1 %collective-permute-start.25 = (f32[32]{0:T(128)S(1)}, f32[32]{0:T(128)S(1)}, u32[]{:S(2)}, u32[]{:S(2)}) collective-permute-start(f32[32]{0:T(128)S(1)} %add_add_fusion.1), channel_id=1, source_target_pairs={{0,1},{1,0},{2,3},{3,2},{4,5},{5,4},{6,7},{7,6},{8,9},{9,8},{10,11... | collective-permute-start | bytes 392 | tf_op jit(solution)/shard_map/ppermute | solution.py:417
  252.3 5.4 %collective-permute-start.26 = (f32[32]{0:T(128)S(1)}, f32[32]{0:T(128)S(1)}, u32[]{:S(2)}, u32[]{:S(2)}) collective-permute-start(f32[32]{0:T(128)S(1)} %add_add_fusion.1), channel_id=1, source_target_pairs={{0,2},{1,3},{2,0},{3,1},{4,6},{5,7},{6,4},{7,5},{8,10},{9,11},{10,... | collective-permute-start | bytes 392 | tf_op jit(solution)/shard_map/ppermute | solution.py:417
  252.3 5.4 %collective-permute-start.27 = (f32[32]{0:T(128)S(1)}, f32[32]{0:T(128)S(1)}, u32[]{:S(2)}, u32[]{:S(2)}) collective-permute-start(f32[32]{0:T(128)S(1)} %add_add_fusion.1), channel_id=1, source_target_pairs={{0,3},{1,2},{2,1},{3,0},{4,7},{5,6},{6,5},{7,4},{8,11},{9,10},{10,... | collective-permute-start | bytes 392 | tf_op jit(solution)/shard_map/ppermute | solution.py:417
  (1 other events, 1.3 us)

commit v3 on v2

--- a/solution.py
+++ b/solution.py
@@ -28,7 +28,7 @@
 
 
 def pack_kernel(experts, meta, outs, eigs, *refs):
-    packed, sems = refs[:experts], refs[experts]
+    packed, tail, sems = refs[:experts], refs[experts], refs[experts + 1]
     depth, width = outs.shape[1], outs.shape[2]
     height = eigs.shape[1]
     chunks = eigs.shape[2] // width
@@ -36,14 +36,25 @@
     for distance in range(experts):
         target = lax.bitwise_xor(meta[2], distance)
         base = distance * (chunks + 1)
+        into, start = packed[distance], depth
+        first = min(depth, into.shape[0])
         copies.append(
-            pltpu.make_async_copy(outs.at[target], packed[distance].at[pl.ds(0, depth), :], sems.at[base])
+            pltpu.make_async_copy(
+                outs.at[target, pl.ds(0, first), :], into.at[pl.ds(0, first), :], sems.at[base]
+            )
         )
+        if first < depth:
+            into, start = tail, depth - first
+            copies.append(
+                pltpu.make_async_copy(
+                    outs.at[target, pl.ds(first, start), :], into.at[pl.ds(0, start), :], sems.at[base + chunks + 1]
+                )
+            )
         for chunk in range(chunks):
             copies.append(
                 pltpu.make_async_copy(
                     eigs.at[target, :, pl.ds(chunk * width, width)],
-                    packed[distance].at[pl.ds(depth + chunk * height, height), :],
+                    into.at[pl.ds(start + chunk * height, height), :],
                     sems.at[base + 1 + chunk],
                 )
             )
@@ -58,12 +69,13 @@
     chunks = eigs.shape[2] // width
     in_hbm = pl.BlockSpec(memory_space=pltpu.HBM)
     shape = jax.ShapeDtypeStruct((depth + chunks * eigs.shape[1], width), F32)
+    half = jax.ShapeDtypeStruct((shape.shape[0] // 2, width), F32)
     return pl.pallas_call(
         functools.partial(pack_kernel, experts),
-        out_shape=[shape] * experts,
+        out_shape=[shape] * (experts - 1) + [half] * 2,
         in_specs=[pl.BlockSpec(memory_space=pltpu.SMEM), in_hbm, in_hbm],
-        out_specs=[pl.BlockSpec(memory_space=pltpu.VMEM)] * experts,
-        scratch_shapes=[pltpu.SemaphoreType.DMA((experts * (chunks + 1),))],
+        out_specs=[pl.BlockSpec(memory_space=pltpu.VMEM)] * (experts + 1),
+        scratch_shapes=[pltpu.SemaphoreType.DMA((experts * (chunks + 1) + 1,))],
         compiler_params=pltpu.CompilerParams(vmem_limit_bytes=32 * 1024 * 1024),
         cost_estimate=pl.CostEstimate(flops=0, bytes_accessed=8 * (outs.size + eigs.size), transcendentals=0),
         name="pack",
@@ -114,6 +126,7 @@
     here_refs = take(2 if fused else 1)
     up_refs, down_refs = take(hops), take(hops)
     own_refs, piece_refs = take(n_own), take(n_piece)
+    tail_refs = take(1 if n_piece else 0)
     in_refs = take(0 if fused else 1)
     earlier = take(2 * planes - 1) if second else None
     sums = take(2 * planes - 1)
@@ -167,10 +180,15 @@
             place(out_copies, out_sems, owns[0], cols.at[:, pl.ds(0, width)])
             place(eig_copies, eig_sems, owns[1], eig.at[pl.ds(0, height), :])
         for index, ref in enumerate(piece_refs, first):
-            place(out_copies, out_sems, ref.at[pl.ds(0, depth), :], cols.at[:, pl.ds(index * width, width)])
+            top, start = min(depth, ref.shape[0]), depth
+            slot = pl.ds(index * width, width)
+            place(out_copies, out_sems, ref.at[pl.ds(0, top), :], cols.at[pl.ds(0, top), slot])
+            if top < depth:
+                ref, start = tail_refs[0], depth - top
+                place(out_copies, out_sems, ref.at[pl.ds(0, start), :], cols.at[pl.ds(top, start), slot])
             for chunk in range(eig.shape[1] // width):
                 spot = eig.at[pl.ds(index * height, height), pl.ds(chunk * width, width)]
-                place(eig_copies, eig_sems, ref.at[pl.ds(depth + chunk * height, height), :], spot)
+                place(eig_copies, eig_sems, ref.at[pl.ds(start + chunk * height, height), :], spot)
         for copy in out_copies:
             copy.start()
 
@@ -277,11 +295,12 @@
     in_hbm = pl.BlockSpec(memory_space=pltpu.HBM)
     sums = [jax.ShapeDtypeStruct((rows, width), F32)] * (2 * planes - 1)
     first_alias = 1 + len(operands) - len(sums)
-    number = len(pieces) + (1 if owns else 0)
+    n_piece = max(0, len(pieces) - 1)
+    number = n_piece + (1 if owns else 0)
     dma = pltpu.SemaphoreType.DMA
     flops = 2 * block * width * (2 * rows * planes + 2 * width)
     results = pl.pallas_call(
-        functools.partial(block_kernel, planes, inner_job, second, len(owns), len(pieces), not inners),
+        functools.partial(block_kernel, planes, inner_job, second, len(owns), n_piece, not inners),
         out_shape=[*sums, jax.ShapeDtypeStruct((1, width), F32)],
         in_specs=[pl.BlockSpec(memory_space=pltpu.SMEM)] + [in_hbm] * len(operands),
         out_specs=[in_hbm] * len(sums) + [pl.BlockSpec(memory_space=pltpu.VMEM)],
@@ -297,7 +316,7 @@
             pltpu.VMEM((block, width), BF16),
             pltpu.VMEM((block, width), BF16),
             pltpu.VMEM((planes, rows, width), F32),
-            dma((number,)),
+            dma((number + 1,)),
             dma((1 + number * max(1, width * number // block),)),
             dma((planes,)),
             dma((planes * number,)),
@@ -382,10 +401,10 @@
         parts = [x if d == 0 else crossing(x, d) for d, x in enumerate(parts)]
         packed = pack(meta, basis_out, eigvals)
         parts, packed = lax.optimization_barrier((parts, packed))
-        pieces = [crossing(packed[d], d) for d in range(1, experts)]
+        pieces = [crossing(x, min(d, experts - 1)) for d, x in enumerate(packed) if d]
         over = [move(x, end_pairs) for x in (packed[0], *pieces)] if any(inward) else []
         part, payload = join([parts, [own, *parts]], packed[-1])
-        below, above = gather(payload, {2: pieces[:-1], 3: [*pieces[-1:], *over[:2]]})
+        below, above = gather(payload, {2: pieces[:-1], 3: [*pieces[-1:], *over[:1]]})
         here_shards = [own, part]
         first_owns, first_pieces, inners = [basis_out, eigvals], pieces, []
     else:

time: 262 us -> 259 us (0.989)
  waiting for transfers between devices: 98.2 us -> 93.6 us
    ppermute x16 -> x17, waiting for transfers between devices: 50.6 us -> 20.9 us  [move(): lax.ppermute(x, ('layer', 'matrix'), [(l * planes + a, l * planes + b) fo...]
    ppermute x16 -> x17, starting transfers between devices: 34.2 us -> 50.9 us  [move(): lax.ppermute(x, ('layer', 'matrix'), [(l * planes + a, l * planes + b) fo...]
    ppermute x6, starting transfers between devices: 88.6 us -> 72.3 us  [shards(): lax.ppermute(scores, axis, [(i, i ^ turn) for i in range(size)])]
    ppermute x6 -> x7, waiting for transfers between devices: 40.7 us -> 56.1 us  [crossing(): lax.ppermute(x, 'expert', [(e, e ^ distance) for e in range(experts)])]
    ppermute x6, waiting for transfers between devices: 6.96 us -> 16.7 us  [shards(): lax.ppermute(scores, axis, [(i, i ^ turn) for i in range(size)])]
    unnamed x42 -> x40, local copies, waits for them, and re-layouts: 6.51 us -> 5.83 us
    ppermute x6 -> x7, starting transfers between devices: 10.1 us -> 9.65 us  [crossing(): lax.ppermute(x, 'expert', [(e, e ^ distance) for e in range(experts)])]
  transfers between devices with their start and end apart: 28 -> 30, of which waited for: 12 -> 11; matrix products, arithmetic and copies ran while one was open for 3% -> 3% of each run, Pallas kernels for 2% -> 2%
where the time goes in v3:
time: 259 us; the launch traced here: 257 us
  starting transfers between devices  133 us (51%)
  waiting for transfers between devices  93.6 us (36%)
  other arithmetic  9.84 us (4%)
  Pallas kernels  8.37 us (3%)
  local copies, waits for them, and re-layouts  8.25 us (3%)
  between operations  3.66 us (1%)
    ppermute x6, starting transfers between devices, shards(): lax.ppermute(scores, axis, [(i, i ^ turn) for i in range(size)])  72.3 us
    ppermute x7, waiting for transfers between devices, crossing(): lax.ppermute(x, 'expert', [(e, e ^ distance) for e in range(experts)])  56.1 us
    ppermute x17, starting transfers between devices, move(): lax.ppermute(x, ('layer', 'matrix'), [(l * planes + a, l * planes + b) fo...  50.9 us
    ppermute x17, waiting for transfers between devices, move(): lax.ppermute(x, ('layer', 'matrix'), [(l * planes + a, l * planes + b) fo...  20.9 us
    ppermute x6, waiting for transfers between devices, shards(): lax.ppermute(scores, axis, [(i, i ^ turn) for i in range(size)])  16.7 us
    ppermute x7, starting transfers between devices, crossing(): lax.ppermute(x, 'expert', [(e, e ^ distance) for e in range(experts)])  9.65 us
    unnamed x40, local copies, waits for them, and re-layouts  5.83 us
  transfers between devices with their start and end apart: 30, of which 11 were waited for; matrix products, arithmetic and copies ran while one was open for 3% of the time, Pallas kernels for 2%

profile of v3, /device:TPU:0, one launch (start us, length us, event | category | flops | bytes accessed | tf_op | source)
XLA Modules:
  0.0 256.6 jit_solution(3033728561435532999)
XLA Ops:
  0.6 1.2 dynamic-slice_bitcast_fusion
  1.8 3.0 %collective-permute-start = (f32[48,768]{1,0:T(8,128)S(1)}, f32[48,768]{1,0:T(8,128)S(1)}, u32[]{:S(2)}, u32[]{:S(2)}) collective-permute-start(f32[48,768]{1,0:T(8,128)S(1)} %get-tuple-element.79), channel_id=1, source_target_pairs={{0,4},{4,0},{8,12},{12,8},{1,5},{5,1},{9,13},{13,9},{2,6},{6,2},{1... | collective-permute-start | bytes 442376 | tf_op jit(solution)/shard_map/ppermute | solution.py:392
  4.8 1.5 collective-permute-start.1
  7.0 1.2 dynamic_slice.16
  9.0 2.2 copy-done
  11.2 1.4 copy-done.2
  12.6 1.6 pack.1
  14.3 1.7 join.1
  16.0 4.1 %collective-permute-start.3 = (f32[704,768]{1,0:T(8,128)S(1)}, f32[704,768]{1,0:T(8,128)S(1)}, u32[]{:S(2)}, u32[]{:S(2)}) collective-permute-start(f32[704,768]{1,0:T(8,128)S(1)} %get-tuple-element.53), channel_id=1, source_target_pairs={{16,17},{17,18},{18,19},{0,1},{1,2},{20,21},{21,22},{22,23},{4,5},... | collective-permute-start | bytes 6488072 | tf_op jit(solution)/shard_map/ppermute | solution.py:351
  20.1 0.8 collective-permute-start.4
  20.9 1.6 collective-permute-start.5
  22.5 1.5 collective-permute-start.6
  24.5 45.7 %collective-permute-done.7.refs_12_ = f32[1408,128]{1,0:T(8,128)S(1)} collective-permute-done((f32[1408,128]{1,0:T(8,128)S(1)}, f32[1408,128]{1,0:T(8,128)S(1)}, u32[]{:S(2)}, u32[]{:S(2)}) %collective-permute-start.7) | collective-permute-done | bytes 720928 | tf_op jit(solution)/shard_map/ppermute | solution.py:392
  70.4 0.8 collective-permute-start.9
  71.2 0.8 collective-permute-start.8
  72.0 4.4 %collective-permute-start.11 = (f32[2816,128]{1,0:T(8,128)S(1)}, f32[2816,128]{1,0:T(8,128)S(1)}, u32[]{:S(2)}, u32[]{:S(2)}) collective-permute-start(f32[2816,128]{1,0:T(8,128)S(1)} %get-tuple-element.59), channel_id=1, source_target_pairs={{0,1},{3,2},{4,5},{7,6},{8,9},{11,10},{12,13},{15,14}} | collective-permute-start | bytes 4325384 | tf_op jit(solution)/shard_map/ppermute | solution.py:351
  76.3 1.6 collective-permute-start.10
  77.9 0.9 broadcast_select_fusion
  78.9 0.9 broadcast_select_fusion.1
  80.2 10.2 %collective-permute-done.10.refs_13_ = f32[1408,128]{1,0:T(8,128)} collective-permute-done((f32[1408,128]{1,0:T(8,128)S(1)}, f32[1408,128]{1,0:T(8,128)}, u32[]{:S(2)}, u32[]{:S(2)}) %collective-permute-start.10) | collective-permute-done | bytes 720928 | tf_op jit(solution)/shard_map/ppermute | solution.py:392
  90.4 2.3 collective-permute-done.11.refs_8_
  92.8 0.8 collective-permute-start.12
  93.6 0.8 collective-permute-start.13
  94.4 8.7 %collective-permute-start.14 = (f32[2816,128]{1,0:T(8,128)S(1)}, f32[2816,128]{1,0:T(8,128)}, u32[]{:S(2)}, u32[]{:S(2)}) collective-permute-start(f32[2816,128]{1,0:T(8,128)S(1)} %collective-permute-done.5.refs_10_), channel_id=1, source_target_pairs={{0,1},{3,2},{4,5},{7,6},{8,9},{11,10},{12,13},{15,14}} | collective-permute-start | bytes 4325384 | tf_op jit(solution)/shard_map/ppermute | solution.py:351
  103.1 2.4 collective-permute-start.15
  105.5 2.1 collective-permute-start.16
  107.7 18.5 %collective-permute-start.17 = (f32[1408,128]{1,0:T(8,128)}, f32[1408,128]{1,0:T(8,128)}, u32[]{:S(2)}, u32[]{:S(2)}) collective-permute-start(f32[1408,128]{1,0:T(8,128)} %collective-permute-done.10.refs_13_), channel_id=1, source_target_pairs={{0,1},{3,2},{4,5},{7,6},{8,9},{11,10},{12,13},{15,14}} | collective-permute-start | bytes 2162696 | tf_op jit(solution)/shard_map/ppermute | solution.py:351
  126.2 1.5 copy-done.15
  127.7 3.2 %first_block.1 = (f32[512,768]{1,0:T(8,128)}, f32[512,768]{1,0:T(8,128)}, f32[512,768]{1,0:T(8,128)}, f32[512,768]{1,0:T(8,128)}, f32[512,768]{1,0:T(8,128)}, /*...) custom-call(s32[4]{0:T(128)} %copy-done.3, f32[512,768]{1,0:T(8,128)} %bitcast.18, f32[192,768]{1,0:T(8,128)} %copy-done.4, ...), custom_call_target="tpu_custom_call" | custom-call | flops 13287555072 | bytes 31457280 | tf_op jit(solution)/shard_map/first_block/pallas_call | solution.py:302
  130.9 10.7 %collective-permute-done.16.refs_11_ = f32[1408,128]{1,0:T(8,128)} collective-permute-done((f32[1408,128]{1,0:T(8,128)S(1)}, f32[1408,128]{1,0:T(8,128)}, u32[]{:S(2)}, u32[]{:S(2)}) %collective-permute-start.16) | collective-permute-done | bytes 720928 | tf_op jit(solution)/shard_map/ppermute | solution.py:351
  141.6 7.8 %collective-permute-done.17.refs_12_ = f32[1408,128]{1,0:T(8,128)} collective-permute-done((f32[1408,128]{1,0:T(8,128)}, f32[1408,128]{1,0:T(8,128)}, u32[]{:S(2)}, u32[]{:S(2)}) %collective-permute-start.17) | collective-permute-done | bytes 720928 | tf_op jit(solution)/shard_map/ppermute | solution.py:351
  149.5 1.8 second_block.1
  152.0 1.0 collective-permute-start.18
  153.1 1.7 add.63
  155.8 0.9 collective-permute-start.19
  157.2 1.4 collective-permute-start.23
  158.7 1.4 add.62
  160.0 1.8 collective-permute-start.20
  163.8 1.3 collective-permute-start.24
  165.1 0.8 collective-permute-start.25
  165.9 1.4 collective-permute-start.26
  167.4 1.3 collective-permute-done.25
  168.7 1.7 collective-permute-done.26
  170.3 66.3 %collective-permute-start.27 = (f32[32]{0:T(128)S(1)}, f32[32]{0:T(128)S(1)}, u32[]{:S(2)}, u32[]{:S(2)}) collective-permute-start(f32[32]{0:T(128)S(1)} %add_add_fusion.1), channel_id=1, source_target_pairs={{0,1},{1,0},{2,3},{3,2},{4,5},{5,4},{6,7},{7,6},{8,9},{9,8},{10,11... | collective-permute-start | bytes 392 | tf_op jit(solution)/shard_map/ppermute | solution.py:436
  236.7 2.4 collective-permute-start.29
  239.1 12.6 %collective-permute-done.27 = f32[32]{0:T(128)S(1)} collective-permute-done((f32[32]{0:T(128)S(1)}, f32[32]{0:T(128)S(1)}, u32[]{:S(2)}, u32[]{:S(2)}) %collective-permute-start.27) | collective-permute-done | bytes 160 | tf_op jit(solution)/shard_map/ppermute | solution.py:436
  251.7 1.1 collective-permute-done.28
  253.3 3.3 %add_bitcast_fusion = f32[1,1,512,768]{3,2,1,0:T(8,128)} fusion(f32[512,768]{1,0:T(8,128)} %get-tuple-element.69, f32[512,768]{1,0:T(8,128)} %collective-permute-done.20, f32[512,768]{1,0:T(8,128)S(1)} %collective-permute-done.23), kind=kLoop, calls=%fused_computation | loop fusion | flops 786432 | bytes 6291456 | tf_op jit(solution)/shard_map/broadcast_in_dim | solution.py:451
  (70 shorter events, 4.6 us)
Async XLA Ops:
  1.8 12.4 %collective-permute-start = (f32[48,768]{1,0:T(8,128)S(1)}, f32[48,768]{1,0:T(8,128)S(1)}, u32[]{:S(2)}, u32[]{:S(2)}) collective-permute-start(f32[48,768]{1,0:T(8,128)S(1)} %get-tuple-element.79), channel_id=1, source_target_pairs={{0,4},{4,0},{8,12},{12,8},{1,5},{5,1},{9,13},{13,9},{2,6},{6,2},{1... | collective-permute-start | bytes 442376 | tf_op jit(solution)/shard_map/ppermute | solution.py:392
  4.8 9.4 %collective-permute-start.1 = (f32[48,768]{1,0:T(8,128)S(1)}, f32[48,768]{1,0:T(8,128)S(1)}, u32[]{:S(2)}, u32[]{:S(2)}) collective-permute-start(f32[48,768]{1,0:T(8,128)S(1)} %get-tuple-element.81), channel_id=1, source_target_pairs={{0,8},{4,12},{8,0},{12,4},{1,9},{5,13},{9,1},{13,5},{2,10},{6,14},... | collective-permute-start | bytes 442376 | tf_op jit(solution)/shard_map/ppermute | solution.py:392
  6.3 7.9 %collective-permute-start.2 = (f32[48,768]{1,0:T(8,128)S(1)}, f32[48,768]{1,0:T(8,128)S(1)}, u32[]{:S(2)}, u32[]{:S(2)}) collective-permute-start(f32[48,768]{1,0:T(8,128)S(1)} %get-tuple-element.78), channel_id=1, source_target_pairs={{0,12},{4,8},{8,4},{12,0},{1,13},{5,9},{9,5},{13,1},{2,14},{6,10},... | collective-permute-start | bytes 442376 | tf_op jit(solution)/shard_map/ppermute | solution.py:392
  9.0 2.2 copy-start
  12.6 1.6 copy-start.3
  12.6 1.7 copy-start.1
  16.0 62.8 %copy-start.4 = (f32[192,768]{1,0:T(8,128)}, f32[192,768]{1,0:T(8,128)S(1)}, u32[]{:S(2)}) copy-start(f32[192,768]{1,0:T(8,128)S(1)} %get-tuple-element.50.refs_1_) | copy-start | bytes 1769476
  16.0 54.3 %collective-permute-start.3 = (f32[704,768]{1,0:T(8,128)S(1)}, f32[704,768]{1,0:T(8,128)S(1)}, u32[]{:S(2)}, u32[]{:S(2)}) collective-permute-start(f32[704,768]{1,0:T(8,128)S(1)} %get-tuple-element.53), channel_id=1, source_target_pairs={{16,17},{17,18},{18,19},{0,1},{1,2},{20,21},{21,22},{22,23},{4,5},... | collective-permute-start | bytes 6488072 | tf_op jit(solution)/shard_map/ppermute | solution.py:351
  20.1 50.2 %collective-permute-start.4 = (f32[704,768]{1,0:T(8,128)S(1)}, f32[704,768]{1,0:T(8,128)S(1)}, u32[]{:S(2)}, u32[]{:S(2)}) collective-permute-start(f32[704,768]{1,0:T(8,128)S(1)} %get-tuple-element.53), channel_id=1, source_target_pairs={{19,18},{18,17},{17,16},{3,2},{2,1},{23,22},{22,21},{21,20},{7,6},... | collective-permute-start | bytes 6488072 | tf_op jit(solution)/shard_map/ppermute | solution.py:351
  20.9 49.3 %collective-permute-start.5 = (f32[2816,128]{1,0:T(8,128)S(1)}, f32[2816,128]{1,0:T(8,128)S(1)}, u32[]{:S(2)}, u32[]{:S(2)}) collective-permute-start(f32[2816,128]{1,0:T(8,128)S(1)} %get-tuple-element.54), channel_id=1, source_target_pairs={{0,4},{4,0},{8,12},{12,8},{1,5},{5,1},{9,13},{13,9},{2,6},{6,2},{1... | collective-permute-start | bytes 4325384 | tf_op jit(solution)/shard_map/ppermute | solution.py:392
  22.5 47.9 %collective-permute-start.6 = (f32[2816,128]{1,0:T(8,128)S(1)}, f32[2816,128]{1,0:T(8,128)S(1)}, u32[]{:S(2)}, u32[]{:S(2)}) collective-permute-start(f32[2816,128]{1,0:T(8,128)S(1)} %get-tuple-element.55), channel_id=1, source_target_pairs={{0,8},{4,12},{8,0},{12,4},{1,9},{5,13},{9,1},{13,5},{2,10},{6,14},... | collective-permute-start | bytes 4325384 | tf_op jit(solution)/shard_map/ppermute | solution.py:392
  24.0 46.2 %collective-permute-start.7 = (f32[1408,128]{1,0:T(8,128)S(1)}, f32[1408,128]{1,0:T(8,128)S(1)}, u32[]{:S(2)}, u32[]{:S(2)}) collective-permute-start(f32[1408,128]{1,0:T(8,128)S(1)} %get-tuple-element.56), channel_id=1, source_target_pairs={{0,12},{4,8},{8,4},{12,0},{1,13},{5,9},{9,5},{13,1},{2,14},{6,10},... | collective-permute-start | bytes 2162696 | tf_op jit(solution)/shard_map/ppermute | solution.py:392
  70.2 35.3 %copy-start.19 = (f32[1408,128]{1,0:T(8,128)}, f32[1408,128]{1,0:T(8,128)S(1)}, u32[]{:S(2)}) copy-start(f32[1408,128]{1,0:T(8,128)S(1)} %collective-permute-done.7.refs_12_) | copy-start | bytes 2162692
  70.2 24.2 %copy-start.16 = (f32[2816,128]{1,0:T(8,128)}, f32[2816,128]{1,0:T(8,128)S(1)}, u32[]{:S(2)}) copy-start(f32[2816,128]{1,0:T(8,128)S(1)} %collective-permute-done.5.refs_10_) | copy-start | bytes 4325380
  70.3 32.8 %copy-start.17 = (f32[2816,128]{1,0:T(8,128)}, f32[2816,128]{1,0:T(8,128)S(1)}, u32[]{:S(2)}) copy-start(f32[2816,128]{1,0:T(8,128)S(1)} %collective-permute-done.6.refs_11_) | copy-start | bytes 4325380
  70.3 8.5 %copy-start.5 = (f32[704,768]{1,0:T(8,128)}, f32[704,768]{1,0:T(8,128)S(1)}, u32[]{:S(2)}) copy-start(f32[704,768]{1,0:T(8,128)S(1)} %collective-permute-done.3.refs_2_) | copy-start | bytes 6488068
  70.3 8.5 %copy-start.6 = (f32[704,768]{1,0:T(8,128)}, f32[704,768]{1,0:T(8,128)S(1)}, u32[]{:S(2)}) copy-start(f32[704,768]{1,0:T(8,128)S(1)} %collective-permute-done.4.refs_5_) | copy-start | bytes 6488068
  70.4 7.5 %collective-permute-start.9 = (f32[704,768]{1,0:T(8,128)S(1)}, f32[704,768]{1,0:T(8,128)S(1)}, u32[]{:S(2)}, u32[]{:S(2)}) collective-permute-start(f32[704,768]{1,0:T(8,128)S(1)} %collective-permute-done.4.refs_5_), channel_id=1, source_target_pairs={{18,17},{17,16},{22,21},{21,20},{26,25},{25,24},{30,29},{29,28}} | collective-permute-start | bytes 6488072 | tf_op jit(solution)/shard_map/ppermute | solution.py:351
  71.2 7.7 %collective-permute-start.8 = (f32[704,768]{1,0:T(8,128)S(1)}, f32[704,768]{1,0:T(8,128)S(1)}, u32[]{:S(2)}, u32[]{:S(2)}) collective-permute-start(f32[704,768]{1,0:T(8,128)S(1)} %collective-permute-done.3.refs_2_), channel_id=1, source_target_pairs={{17,18},{18,19},{21,22},{22,23},{25,26},{26,27},{29,30},{30,31}} | collective-permute-start | bytes 6488072 | tf_op jit(solution)/shard_map/ppermute | solution.py:351
  72.0 20.8 %collective-permute-start.11 = (f32[2816,128]{1,0:T(8,128)S(1)}, f32[2816,128]{1,0:T(8,128)S(1)}, u32[]{:S(2)}, u32[]{:S(2)}) collective-permute-start(f32[2816,128]{1,0:T(8,128)S(1)} %get-tuple-element.59), channel_id=1, source_target_pairs={{0,1},{3,2},{4,5},{7,6},{8,9},{11,10},{12,13},{15,14}} | collective-permute-start | bytes 4325384 | tf_op jit(solution)/shard_map/ppermute | solution.py:351
  76.3 14.1 %collective-permute-start.10 = (f32[1408,128]{1,0:T(8,128)S(1)}, f32[1408,128]{1,0:T(8,128)}, u32[]{:S(2)}, u32[]{:S(2)}) collective-permute-start(f32[1408,128]{1,0:T(8,128)S(1)} %get-tuple-element.45.refs_0_), channel_id=1, source_target_pairs={{0,12},{4,8},{8,4},{12,0},{1,13},{5,9},{9,5},{13,1},{2,14},{6,10},... | collective-permute-start | bytes 2162696 | tf_op jit(solution)/shard_map/ppermute | solution.py:392
  77.9 1.9 copy-start.7
  92.8 33.4 %copy-start.18 = (f32[2816,128]{1,0:T(8,128)}, f32[2816,128]{1,0:T(8,128)S(1)}, u32[]{:S(2)}) copy-start(f32[2816,128]{1,0:T(8,128)S(1)} %collective-permute-done.11.refs_8_) | copy-start | bytes 4325380
  92.8 14.9 %collective-permute-start.12 = (f32[704,768]{1,0:T(8,128)S(1)}, f32[704,768]{1,0:T(8,128)S(1)}, u32[]{:S(2)}, u32[]{:S(2)}) collective-permute-start(f32[704,768]{1,0:T(8,128)S(1)} %broadcast_select_fusion.1), channel_id=1, source_target_pairs={{18,19},{1,2},{22,23},{5,6},{26,27},{9,10},{30,31},{13,14}} | collective-permute-start | bytes 6488072 | tf_op jit(solution)/shard_map/ppermute | solution.py:351
  93.6 32.6 %collective-permute-start.13 = (f32[704,768]{1,0:T(8,128)S(1)}, f32[704,768]{1,0:T(8,128)S(1)}, u32[]{:S(2)}, u32[]{:S(2)}) collective-permute-start(f32[704,768]{1,0:T(8,128)S(1)} %broadcast_select_fusion), channel_id=1, source_target_pairs={{17,16},{2,1},{21,20},{6,5},{25,24},{10,9},{29,28},{14,13}} | collective-permute-start | bytes 6488072 | tf_op jit(solution)/shard_map/ppermute | solution.py:351
  94.4 55.1 %collective-permute-start.14 = (f32[2816,128]{1,0:T(8,128)S(1)}, f32[2816,128]{1,0:T(8,128)}, u32[]{:S(2)}, u32[]{:S(2)}) collective-permute-start(f32[2816,128]{1,0:T(8,128)S(1)} %collective-permute-done.5.refs_10_), channel_id=1, source_target_pairs={{0,1},{3,2},{4,5},{7,6},{8,9},{11,10},{12,13},{15,14}} | collective-permute-start | bytes 4325384 | tf_op jit(solution)/shard_map/ppermute | solution.py:351
  103.1 46.3 %collective-permute-start.15 = (f32[2816,128]{1,0:T(8,128)S(1)}, f32[2816,128]{1,0:T(8,128)}, u32[]{:S(2)}, u32[]{:S(2)}) collective-permute-start(f32[2816,128]{1,0:T(8,128)S(1)} %collective-permute-done.6.refs_11_), channel_id=1, source_target_pairs={{0,1},{3,2},{4,5},{7,6},{8,9},{11,10},{12,13},{15,14}} | collective-permute-start | bytes 4325384 | tf_op jit(solution)/shard_map/ppermute | solution.py:351
  105.5 36.1 %collective-permute-start.16 = (f32[1408,128]{1,0:T(8,128)S(1)}, f32[1408,128]{1,0:T(8,128)}, u32[]{:S(2)}, u32[]{:S(2)}) collective-permute-start(f32[1408,128]{1,0:T(8,128)S(1)} %collective-permute-done.7.refs_12_), channel_id=1, source_target_pairs={{0,1},{3,2},{4,5},{7,6},{8,9},{11,10},{12,13},{15,14}} | collective-permute-start | bytes 2162696 | tf_op jit(solution)/shard_map/ppermute | solution.py:351
  107.7 18.5 %copy-start.14 = (f32[704,768]{1,0:T(8,128)}, f32[704,768]{1,0:T(8,128)S(1)}, u32[]{:S(2)}) copy-start(f32[704,768]{1,0:T(8,128)S(1)} %collective-permute-done.12.refs_4_) | copy-start | bytes 6488068
  107.7 41.8 %collective-permute-start.17 = (f32[1408,128]{1,0:T(8,128)}, f32[1408,128]{1,0:T(8,128)}, u32[]{:S(2)}, u32[]{:S(2)}) collective-permute-start(f32[1408,128]{1,0:T(8,128)} %collective-permute-done.10.refs_13_), channel_id=1, source_target_pairs={{0,1},{3,2},{4,5},{7,6},{8,9},{11,10},{12,13},{15,14}} | collective-permute-start | bytes 2162696 | tf_op jit(solution)/shard_map/ppermute | solution.py:351
  126.2 1.5 copy-start.15
  151.3 1.8 collective-permute-start.21
  152.0 3.6 %collective-permute-start.18 = (f32[512,768]{1,0:T(8,128)}, f32[512,768]{1,0:T(8,128)S(1)}, u32[]{:S(2)}, u32[]{:S(2)}) collective-permute-start(f32[512,768]{1,0:T(8,128)} %get-tuple-element.72), channel_id=1, source_target_pairs={{16,17},{20,21},{24,25},{28,29}} | collective-permute-start | bytes 4718600 | tf_op jit(solution)/shard_map/ppermute | solution.py:351
  153.1 2.5 copy-start.11
  154.8 1.9 collective-permute-start.22
  155.6 1.4 copy-start.9
  155.8 2.8 %collective-permute-start.19 = (f32[512,768]{1,0:T(8,128)S(1)}, f32[512,768]{1,0:T(8,128)S(1)}, u32[]{:S(2)}, u32[]{:S(2)}) collective-permute-start(f32[512,768]{1,0:T(8,128)S(1)} %add.61), channel_id=1, source_target_pairs={{1,2},{16,17},{17,18},{5,6},{20,21},{21,22},{9,10},{24,25},{25,26}... | collective-permute-start | bytes 4718600 | tf_op jit(solution)/shard_map/ppermute | solution.py:351
  157.0 1.6 copy-start.10
  157.2 96.1 %collective-permute-start.23 = (f32[512,768]{1,0:T(8,128)S(1)}, f32[512,768]{1,0:T(8,128)S(1)}, u32[]{:S(2)}, u32[]{:S(2)}) collective-permute-start(f32[512,768]{1,0:T(8,128)S(1)} %add.64), channel_id=1, source_target_pairs={{2,1},{1,0},{19,18},{18,17},{17,16},{6,5},{5,4},{23,22},{22,21},{2... | collective-permute-start | bytes 4718600 | tf_op jit(solution)/shard_map/ppermute | solution.py:351
  158.7 3.8 %copy-start.12 = (f32[1,768]{1,0:T(1,128)S(1)}, f32[1,768]{1,0:T(1,128)}, u32[]{:S(2)}) copy-start(f32[1,768]{1,0:T(1,128)} %get-tuple-element.76) | copy-start | bytes 9220
  158.7 3.8 %copy-start.13 = (f32[1,768]{1,0:T(1,128)S(1)}, f32[1,768]{1,0:T(1,128)}, u32[]{:S(2)}) copy-start(f32[1,768]{1,0:T(1,128)} %get-tuple-element.77) | copy-start | bytes 9220
  160.0 93.3 %collective-permute-start.20 = (f32[512,768]{1,0:T(8,128)}, f32[512,768]{1,0:T(8,128)}, u32[]{:S(2)}, u32[]{:S(2)}) collective-permute-start(f32[512,768]{1,0:T(8,128)} %add.62), channel_id=1, source_target_pairs={{1,2},{2,3},{16,17},{17,18},{18,19},{5,6},{6,7},{20,21},{21,22},{2... | collective-permute-start | bytes 4718600 | tf_op jit(solution)/shard_map/ppermute | solution.py:351
  163.8 3.6 %collective-permute-start.24 = (f32[32]{0:T(128)S(1)}, f32[32]{0:T(128)S(1)}, u32[]{:S(2)}, u32[]{:S(2)}) collective-permute-start(f32[32]{0:T(128)S(1)} %compare_select_fusion), channel_id=1, source_target_pairs={{0,4},{4,0},{8,12},{12,8},{1,5},{5,1},{9,13},{13,9},{2,6},{6,2},{1... | collective-permute-start | bytes 392 | tf_op jit(solution)/shard_map/ppermute | solution.py:436
  165.1 3.5 %collective-permute-start.25 = (f32[32]{0:T(128)S(1)}, f32[32]{0:T(128)S(1)}, u32[]{:S(2)}, u32[]{:S(2)}) collective-permute-start(f32[32]{0:T(128)S(1)} %compare_select_fusion), channel_id=1, source_target_pairs={{0,8},{4,12},{8,0},{12,4},{1,9},{5,13},{9,1},{13,5},{2,10},{6,14},... | collective-permute-start | bytes 392 | tf_op jit(solution)/shard_map/ppermute | solution.py:436
  165.9 4.4 %collective-permute-start.26 = (f32[32]{0:T(128)S(1)}, f32[32]{0:T(128)S(1)}, u32[]{:S(2)}, u32[]{:S(2)}) collective-permute-start(f32[32]{0:T(128)S(1)} %compare_select_fusion), channel_id=1, source_target_pairs={{0,12},{4,8},{8,4},{12,0},{1,13},{5,9},{9,5},{13,1},{2,14},{6,10},... | collective-permute-start | bytes 392 | tf_op jit(solution)/shard_map/ppermute | solution.py:436
  170.3 81.3 %collective-permute-start.27 = (f32[32]{0:T(128)S(1)}, f32[32]{0:T(128)S(1)}, u32[]{:S(2)}, u32[]{:S(2)}) collective-permute-start(f32[32]{0:T(128)S(1)} %add_add_fusion.1), channel_id=1, source_target_pairs={{0,1},{1,0},{2,3},{3,2},{4,5},{5,4},{6,7},{7,6},{8,9},{9,8},{10,11... | collective-permute-start | bytes 392 | tf_op jit(solution)/shard_map/ppermute | solution.py:436
  236.7 16.1 %collective-permute-start.28 = (f32[32]{0:T(128)S(1)}, f32[32]{0:T(128)S(1)}, u32[]{:S(2)}, u32[]{:S(2)}) collective-permute-start(f32[32]{0:T(128)S(1)} %add_add_fusion.1), channel_id=1, source_target_pairs={{0,2},{1,3},{2,0},{3,1},{4,6},{5,7},{6,4},{7,5},{8,10},{9,11},{10,... | collective-permute-start | bytes 392 | tf_op jit(solution)/shard_map/ppermute | solution.py:436
  236.7 16.1 %collective-permute-start.29 = (f32[32]{0:T(128)S(1)}, f32[32]{0:T(128)S(1)}, u32[]{:S(2)}, u32[]{:S(2)}) collective-permute-start(f32[32]{0:T(128)S(1)} %add_add_fusion.1), channel_id=1, source_target_pairs={{0,3},{1,2},{2,1},{3,0},{4,7},{5,6},{6,5},{7,4},{8,11},{9,10},{10,... | collective-permute-start | bytes 392 | tf_op jit(solution)/shard_map/ppermute | solution.py:436
  (2 other events, 2.8 us)
